TPU v7x, 128 devices: a whole 4x4x4 slice. The times are simulated.
128 devices in a mesh: ax: 8 (over z, core), xs: 16 (over x, y).
Axes of the slice: x: 4, y: 4, z: 4, core: 2. Of those that a mesh axis runs over, the one named last changes fastest.
Arguments:
- flow_vector: bfloat16 [3, 16, 64, 32, 512], P(None, 'ax', 'xs'), may hold values from -6 to 6
- thermal_state: bfloat16 [16, 64, 32, 512], P('ax', 'xs'), may hold values from 0.5 to 1.5
- stiffness_weights: float32 [3, 16, 64, 32, 512], P(None, 'ax', 'xs'), may hold values from 0.002 to 0.02
- inertia_over_timestep: float32 [16, 64, 32, 512], P('ax', 'xs'), may hold values from 0.1 to 1
- tracer_interval_index: int32 [3, 524288], P(None, ('ax', 'xs')), may hold values from 0 to 6
- tracer_interval_offset: float32 [3, 524288], P(None, ('ax', 'xs')), may hold values from 0 to 1
- tracer_holding_chip: int32 [524288, 1], P(('ax', 'xs')), may hold values from 0 to 127; in each aligned block of 4096 rows (0 to 4095, 4096 to 8191, ...) at most 128 rows name the same one
- tracer_containing_piece: int32 [524288], P(('ax', 'xs')), may hold values from 0 to 255
- chemical_shares: float32 [6, 524288], P(None, ('ax', 'xs')), may hold values from 0.2 to 1
- frequency_scale: float32 [6], replicated, may hold values from 0.5 to 2
- energy_barrier: float32 [6], replicated, may hold values from 0.5 to 2
Outputs:
- velocity_out: float32 [3, 16, 64, 32, 512], P(None, 'ax', 'xs')
- coords_new: float32 [3, 524288], P(None, ('ax', 'xs'))
- species_new: float32 [6, 524288], P(None, ('ax', 'xs'))
Inputs may be any that keep to these rules, and one draw needn't show every extreme that they name: `tracer_holding_chip`: among the particles of one device, at most 128 name the same owner device, and this bound is reached.
All inputs are finite; a program needn't handle non-finite values.
Results may differ from a plain program's by a relative error of at most 0.0003.
Values sent between devices are 32-bit elements; how exact they have to be, the bound alone decides.
A program may use at most 128 MiB of HBM per device.

v0:
```python
import functools

import jax
import jax.numpy as jnp
import numpy as np
from jax import lax
from jax.experimental import pallas as pl
from jax.experimental.pallas import tpu as pltpu
from jax.sharding import PartitionSpec as P

NODE_LIST = (
    -1.0,
    -0.8717401485096066,
    -0.5917001814331423,
    -0.2092992179024789,
    0.2092992179024789,
    0.5917001814331423,
    0.8717401485096066,
    1.0,
)
STEP_DT = 0.25
F32 = jnp.float32
BF16 = jnp.bfloat16
CHUNK = 256


def bary_weights():
    nodes = np.array(NODE_LIST)
    weights = np.zeros(8)
    for a in range(8):
        weights[a] = 1.0 / np.prod([nodes[a] - nodes[m] for m in range(8) if m != a])
    return nodes, weights


def deriv_table():
    nodes, weights = bary_weights()
    table = np.zeros((8, 8))
    for row in range(8):
        for col in range(8):
            if row != col:
                table[row, col] = weights[col] / weights[row] / (nodes[row] - nodes[col])
        table[row, row] = -np.sum(table[row])
    return table


DM = np.asarray(deriv_table(), np.float32).astype(np.float64)


def roll_tables():
    out = np.zeros((16, 8, 128), np.float32)
    for half, table in enumerate((DM, DM.T)):
        for s in range(8):
            for p in range(8):
                out[half * 8 + s, p, :] = table[p, (p - s) % 8]
    return out


def apply_table(table, u):
    even = [u[i] + u[7 - i] for i in range(4)]
    odd = [u[i] - u[7 - i] for i in range(4)]
    out = [None] * 8
    for p in range(4):
        a = b = None
        for i in range(4):
            ca = float((table[p, i] + table[p, 7 - i]) / 2)
            cb = float((table[p, i] - table[p, 7 - i]) / 2)
            ta, tb = even[i] * ca, odd[i] * cb
            a = ta if a is None else a + ta
            b = tb if b is None else b + tb
        out[p], out[7 - p] = a + b, b - a
    return out


def apply_rolls(tables, x):
    y = x * tables[0]
    for s in range(1, 8):
        y = y + pltpu.roll(x, s, 0) * tables[s]
    return y


def pick_node(cell, shift):
    out = jnp.full(cell.shape, NODE_LIST[shift], F32)
    for c in range(1, 7):
        out = jnp.where(cell == c, F32(NODE_LIST[c + shift]), out)
    return out


def split(x):
    high = x.astype(BF16).astype(F32)
    return high, x - high


def dispatch(idx_ref, off_ref, own_ref, piece_ref, coords_ref, rank_ref, pay_ref):
    total = idx_ref.shape[1]
    cell = idx_ref[...]
    low, high = pick_node(cell, 0), pick_node(cell, 1)
    coords_ref[...] = low + off_ref[...] * (high - low)
    rows = lax.broadcasted_iota(jnp.int32, (CHUNK, 2 * CHUNK), 0)
    cols = lax.broadcasted_iota(jnp.int32, (CHUNK, 2 * CHUNK), 1)
    before = jnp.where((rows < cols) | (cols >= CHUNK), 1.0, 0.0).astype(BF16)
    lane_id = lax.broadcasted_iota(jnp.int32, (128, CHUNK), 0)
    base = jnp.zeros((128, CHUNK), F32)
    for c in range(total // CHUNK):
        part = pl.ds(c * CHUNK, CHUNK)
        hot = jnp.where(own_ref[:, part] == lane_id, 1.0, 0.0)
        count = jnp.dot(hot.astype(BF16), before, preferred_element_type=F32)
        rank = jnp.sum(hot * (count[:, :CHUNK] + base), axis=0, keepdims=True)
        rank_ref[:, part] = rank.astype(jnp.int32)
        base = base + count[:, CHUNK:]
    pay_ref[...] = jnp.zeros_like(pay_ref)
    dims = (((1,), (1,)), ((), ()))
    for c in range(total // CHUNK):
        part = pl.ds(c * CHUNK, CHUNK)
        hot = jnp.where(own_ref[:, part] == lane_id, 1.0, 0.0).astype(BF16)
        mask = rank_ref[:, part] == lane_id
        tops, lows = [], []
        for d in range(3):
            high, rest = split(coords_ref[pl.ds(d, 1), part])
            tops.append(jnp.where(mask, high, 0.0).astype(BF16))
            lows.append(jnp.where(mask, rest, 0.0).astype(BF16))
        tops.append(jnp.where(mask, piece_ref[:, part].astype(F32), 0.0).astype(BF16))
        one = lax.dot_general(hot, jnp.concatenate(tops, 0), dims, preferred_element_type=F32)
        two = lax.dot_general(hot, jnp.concatenate(lows, 0), dims, preferred_element_type=F32)
        pay_ref[:, :384] += one[:, :384] + two
        pay_ref[:, 384:] += one[:, 384:]


def interpolate(got_ref, table_ref, back_ref, lag_ref, rows_ref):
    nodes, weights = bary_weights()
    ident = lax.broadcasted_iota(jnp.int32, (256, 256), 0)

    def block(b, carry):
        base = pl.multiple_of(b * 8, 8)
        for d in range(3):
            x = got_ref[pl.ds(base, 8), d * 128 : (d + 1) * 128]
            diff = [x - F32(n) for n in nodes]
            ahead, behind = [None] * 8, [None] * 8
            ahead[1], behind[6] = diff[0], diff[7]
            for i in range(2, 8):
                ahead[i] = ahead[i - 1] * diff[i - 1]
                behind[7 - i] = behind[8 - i] * diff[8 - i]
            for i in range(8):
                prod = behind[0] if i == 0 else ahead[7] if i == 7 else ahead[i] * behind[i]
                lag_ref[pl.ds(d * 64 + i * 8, 8), :] = prod * F32(weights[i])
        elem = got_ref[pl.ds(base, 8), 384:512].astype(jnp.int32)
        for pair in range(4):
            s0, s1 = 2 * pair, 2 * pair + 1
            ids = jnp.concatenate([elem[s0 : s0 + 1], elem[s1 : s1 + 1]], 1)
            hot = jnp.where(ident == ids, 1.0, 0.0).astype(BF16)

            def weight(d, i):
                row = d * 64 + i * 8
                return jnp.concatenate(
                    [lag_ref[pl.ds(row + s0, 1), :], lag_ref[pl.ds(row + s1, 1), :]], 1
                )

            third = jnp.concatenate(
                [lag_ref[pl.ds(128 + s0, 8, stride=8), :], lag_ref[pl.ds(128 + s1, 8, stride=8), :]], 1
            )
            for f in range(4):
                rows = jnp.dot(
                    table_ref[pl.ds(f * 512, 512), :], hot, preferred_element_type=F32
                )
                one = None
                for i in range(8):
                    term = rows[i * 64 : (i + 1) * 64] * weight(0, i)
                    one = term if one is None else one + term
                two = None
                for j in range(8):
                    term = one[j * 8 : (j + 1) * 8] * weight(1, j)
                    two = term if two is None else two + term
                value = jnp.sum(two * third, axis=0, keepdims=True)
                rows_ref[s0 : s0 + 1, f * 128 : (f + 1) * 128] = value[:, :128]
                rows_ref[s1 : s1 + 1, f * 128 : (f + 1) * 128] = value[:, 128:]
        back_ref[pl.ds(base, 8), :] = rows_ref[...]
        return carry

    lax.fori_loop(0, got_ref.shape[0] // 8, block, 0)


def combine(ret_ref, own_ref, rank_ref, coords_ref, share_ref, freq_ref, barrier_ref, cnew_ref, snew_ref, halves_ref):
    total = own_ref.shape[1]
    for f in range(4):
        turned = jnp.transpose(ret_ref[:, f * 128 : (f + 1) * 128])
        high, rest = split(turned)
        halves_ref[pl.ds(f * 128, 128), 0:128] = high.astype(BF16)
        halves_ref[pl.ds(f * 128, 128), 128:256] = rest.astype(BF16)
    lane_id = lax.broadcasted_iota(jnp.int32, (128, CHUNK), 0)
    freq, barrier = freq_ref[...], barrier_ref[...]
    for c in range(total // CHUNK):
        part = pl.ds(c * CHUNK, CHUNK)
        hot = jnp.where(own_ref[:, part] == lane_id, 1.0, 0.0).astype(BF16)
        found = jnp.dot(
            halves_ref[...], jnp.concatenate([hot, hot], 0), preferred_element_type=F32
        )
        mask = rank_ref[:, part] == lane_id
        probe = [
            jnp.sum(jnp.where(mask, found[f * 128 : (f + 1) * 128], 0.0), axis=0, keepdims=True)
            for f in range(4)
        ]
        for d in range(3):
            cnew_ref[pl.ds(d, 1), part] = coords_ref[pl.ds(d, 1), part] + STEP_DT * probe[d]
        rates = freq * jnp.exp(barrier * jnp.tanh(probe[3] - 1.0))
        shares = share_ref[:, part]
        flux = rates * shares
        moved = jnp.concatenate([flux[5:6], flux[0:5]], 0)
        snew_ref[:, part] = shares + STEP_DT * (moved - flux)


def turn_in(flow_ref, heat_ref, stiff_ref, inert_ref, x_ref, table_ref, g_ref, c_ref):
    def three(d, carry):
        for a in range(2):
            lanes = pl.ds(a * 128, 128)
            turned = jnp.transpose(flow_ref[d, lanes, :].astype(F32))
            x_ref[d, :, lanes] = turned
            table_ref[pl.ds(pl.multiple_of(d * 512, 512), 512), lanes] = turned.astype(BF16)
            g_ref[d, :, lanes] = jnp.transpose(stiff_ref[d, lanes, :])
        return carry

    lax.fori_loop(0, 3, three, 0)
    for a in range(2):
        lanes = pl.ds(a * 128, 128)
        table_ref[pl.ds(1536, 512), lanes] = jnp.transpose(heat_ref[lanes, :].astype(F32)).astype(BF16)
        c_ref[:, lanes] = jnp.transpose(inert_ref[lanes, :])


def helm(x_ref, g_ref, c_ref, t_ref, h_ref):
    def part(n, carry):
        f, a = n // 2, n % 2
        lanes = pl.ds(pl.multiple_of(a * 128, 128), 128)
        fore = [t_ref[s] for s in range(8)]
        aft = [t_ref[8 + s] for s in range(8)]
        for i in range(8):
            at = [pl.ds(i * 64 + j * 8, 8) for j in range(8)]
            x = [x_ref[f, at[j], lanes] for j in range(8)]
            dj = apply_table(DM, x)
            dj = [g_ref[1, at[j], lanes] * dj[j] for j in range(8)]
            dj = apply_table(DM.T, dj)
            for j in range(8):
                dk = g_ref[2, at[j], lanes] * apply_rolls(fore, x[j])
                h_ref[f, at[j], lanes] = dj[j] + c_ref[at[j], lanes] * x[j] + apply_rolls(aft, dk)
        for j in range(8):
            at = [pl.ds(i * 64 + j * 8, 8) for i in range(8)]
            di = apply_table(DM, [x_ref[f, at[i], lanes] for i in range(8)])
            di = [g_ref[0, at[i], lanes] * di[i] for i in range(8)]
            di = apply_table(DM.T, di)
            for i in range(8):
                h_ref[f, at[i], lanes] += di[i]
        return carry

    lax.fori_loop(0, 6, part, 0)


def faces(h_ref, low_ref, high_ref, left_ref, right_ref):
    for f in range(3):
        low_ref[f] = h_ref[f, 0:64, 0:128]
        high_ref[f] = h_ref[f, 448:512, 128:256]
        both = h_ref[f, 448:512, 0:128] + h_ref[f, 0:64, 128:256]
        h_ref[f, 448:512, 0:128] = both
        h_ref[f, 0:64, 128:256] = both
    lane = lax.broadcasted_iota(jnp.int32, (8, 128), 1) // 32

    def pack(n, carry):
        f, a = n // 2, n % 2
        lanes = pl.ds(pl.multiple_of(a * 128, 128), 128)
        for half in range(2):
            one = two = None
            for q in range(4):
                row = (half * 4 + q) * 64
                first = h_ref[f, pl.ds(row, 8), lanes]
                last = h_ref[f, pl.ds(row + 56, 8), lanes]
                if q:
                    first = pltpu.roll(first, 32 * q, 1)
                if q < 3:
                    last = pltpu.roll(last, 32 * q + 32, 1)
                one = first if one is None else jnp.where(lane == q, first, one)
                two = last if two is None else jnp.where(lane == q, last, two)
            left_ref[f, a, half] = one
            right_ref[f, a, half] = two
        return carry

    lax.fori_loop(0, 6, pack, 0)


def assemble(h_ref, x_ref, low_ref, high_ref, left_ref, right_ref, corner):
    lane = lax.broadcasted_iota(jnp.int32, (8, 128), 1)
    sub = lax.broadcasted_iota(jnp.int32, (8, 128), 0)
    quarter, radial = lane // 32, lane % 32
    at_first = (sub == 0) & (radial != 0)
    at_last = (sub == 7) & (radial != 31)

    def near(f, carry):
        h_ref[f, 0:64, 0:128] += low_ref[f]
        h_ref[f, 448:512, 128:256] += high_ref[f]
        left_ref[f, 0, 0] += jnp.where(quarter == 0, pltpu.roll(corner(0)[f], 32, 1), 0.0)
        left_ref[f, 1, 1] += jnp.where(quarter == 3, pltpu.roll(corner(1)[f], 96, 1), 0.0)
        right_ref[f, 0, 0] += jnp.where(quarter == 0, pltpu.roll(corner(2)[f], 32, 1), 0.0)
        right_ref[f, 1, 1] += jnp.where(quarter == 3, pltpu.roll(corner(3)[f], 96, 1), 0.0)
        return carry

    lax.fori_loop(0, 3, near, 0)

    def radially(x):
        up = pltpu.roll(pltpu.roll(x, 1, 1), 1, 0)
        down = pltpu.roll(pltpu.roll(x, 127, 1), 7, 0)
        return x + jnp.where(at_first, up, 0.0) + jnp.where(at_last, down, 0.0)

    def part(n, carry):
        f, a = n // 2, n % 2
        lanes = pl.ds(pl.multiple_of(a * 128, 128), 128)
        for i in range(8):
            half, q = i // 4, i % 4
            first = h_ref[f, pl.ds(i * 64, 8), lanes]
            last = h_ref[f, pl.ds(i * 64 + 56, 8), lanes]
            before, after = left_ref[f, a, half], right_ref[f, a, half]
            if q:
                before = pltpu.roll(before, 128 - 32 * q, 1)
            if q < 3:
                after = pltpu.roll(after, 96 - 32 * q, 1)
            before = jnp.where(quarter == 0, before, pltpu.roll(last, 32, 1))
            after = jnp.where(quarter == 3, after, pltpu.roll(first, 96, 1))
            x_ref[f, pl.ds(i * 64, 8), lanes] = radially(first + before)
            x_ref[f, pl.ds(i * 64 + 56, 8), lanes] = radially(last + after)
            for j in range(1, 7):
                row = pl.ds(i * 64 + j * 8, 8)
                x_ref[f, row, lanes] = radially(h_ref[f, row, lanes])
        return carry

    lax.fori_loop(0, 6, part, 0)


def turn_out(x_ref, out_ref):
    def three(d, carry):
        for a in range(2):
            lanes = pl.ds(a * 128, 128)
            out_ref[d, lanes, :] = jnp.transpose(x_ref[d, :, lanes])
        return carry

    lax.fori_loop(0, 3, three, 0)


def call(body, outs, scratch, *args):
    vmem = pl.BlockSpec(memory_space=pltpu.VMEM)
    return pl.pallas_call(
        body,
        out_shape=[jax.ShapeDtypeStruct(shape, dtype) for shape, dtype in outs],
        in_specs=[vmem] * len(args),
        out_specs=[vmem] * len(outs),
        scratch_shapes=[pltpu.VMEM(shape, dtype) for shape, dtype in scratch],
        compiler_params=pltpu.CompilerParams(vmem_limit_bytes=48 * 1024 * 1024),
    )(*args)


FIELD = ((3, 512, 256), F32)
FACE = ((3, 64, 128), F32)
SIDE = ((3, 2, 2, 8, 128), F32)
FACES = [FACE, FACE, SIDE, SIDE]


def first_body(flow, heat, stiff, inert, tables, h, table, g, c, low, high, left, right, x):
    turn_in(flow, heat, stiff, inert, x, table, g, c)
    helm(x, g, c, tables, h)
    faces(h, low, high, left, right)


def second_body(h1, g, c, tables, low1, high1, left1, right1, corners, h, low, high, left, right, x, work, l1, r1):
    work[...] = h1[...]
    l1[...] = left1[...]
    r1[...] = right1[...]
    assemble(work, x, low1, high1, l1, r1, lambda n: corners.at[n])
    helm(x, g, c, tables, h)
    faces(h, low, high, left, right)


def last_body(h1, low1, high1, left1, right1, corners, out, x, work, l1, r1):
    work[...] = h1[...]
    l1[...] = left1[...]
    r1[...] = right1[...]
    assemble(work, x, low1, high1, l1, r1, lambda n: corners.at[n])
    turn_out(x, out)


def exchange(low, high, left, right):
    n_ax, n_xs = lax.axis_size("ax"), lax.axis_size("xs")

    def shift(value, da, dx):
        if da == 0:
            pairs = [(i, (i + dx) % n_xs) for i in range(n_xs)]
            return lax.ppermute(value, "xs", pairs)
        if dx == 0:
            pairs = [(i, i + da) for i in range(n_ax) if 0 <= i + da < n_ax]
            return lax.ppermute(value, "ax", pairs)
        pairs = [
            (i * n_xs + j, (i + da) * n_xs + (j + dx) % n_xs)
            for i in range(n_ax)
            for j in range(n_xs)
            if 0 <= i + da < n_ax
        ]
        return lax.ppermute(value, ("ax", "xs"), pairs)

    corners = jnp.stack(
        [
            shift(right[:, 1, 1], 1, 1),
            shift(right[:, 0, 0], -1, 1),
            shift(left[:, 1, 1], 1, -1),
            shift(left[:, 0, 0], -1, -1),
        ]
    )
    return shift(high, 1, 0), shift(low, -1, 0), shift(right, 0, 1), shift(left, 0, -1), corners


def local(flow, heat, stiff, inert, index, offset, owner, piece, shares, freq, barrier):
    particles = piece.shape[0]
    flow3 = flow.reshape(3, 256, 512)
    heat2 = heat.reshape(256, 512)
    stiff3 = stiff.reshape(3, 256, 512)
    inert2 = inert.reshape(256, 512)
    owner = owner.reshape(1, particles)
    piece = piece.reshape(1, particles)
    tables = jnp.asarray(roll_tables())
    coords, rank, payload = call(
        dispatch,
        [((3, particles), F32), ((1, particles), jnp.int32), ((128, 512), F32)],
        [],
        index,
        offset,
        owner,
        piece,
    )
    received = lax.all_to_all(payload, ("ax", "xs"), split_axis=0, concat_axis=0, tiled=True)
    h, table, g, c, *rims = call(
        first_body,
        [FIELD, ((2048, 256), BF16), FIELD, ((512, 256), F32)] + FACES,
        [FIELD],
        flow3,
        heat2,
        stiff3,
        inert2,
        tables,
    )
    rims = exchange(*rims)
    (values,) = call(interpolate, [((128, 512), F32)], [((192, 128), F32), ((8, 512), F32)], received, table)
    returned = lax.all_to_all(values, ("ax", "xs"), split_axis=0, concat_axis=0, tiled=True)
    h, *rims = call(
        second_body, [FIELD] + FACES, [FIELD, FIELD, SIDE, SIDE], h, g, c, tables, *rims
    )
    rims = exchange(*rims)
    cnew, snew = call(
        combine,
        [((3, particles), F32), ((6, particles), F32)],
        [((512, 256), BF16)],
        returned,
        owner,
        rank,
        coords,
        shares,
        freq.reshape(6, 1),
        barrier.reshape(6, 1),
    )
    (out,) = call(last_body, [((3, 256, 512), F32)], [FIELD, FIELD, SIDE, SIDE], h, *rims)
    return out.reshape(flow.shape), cnew, snew


def solution(mesh):
    placed = (
        P(None, "ax", "xs", None, None),
        P("ax", "xs", None, None),
        P(None, "ax", "xs", None, None),
        P("ax", "xs", None, None),
        P(None, ("ax", "xs")),
        P(None, ("ax", "xs")),
        P(("ax", "xs"), None),
        P(("ax", "xs")),
        P(None, ("ax", "xs")),
        P(),
        P(),
    )
    return jax.shard_map(
        local,
        mesh=mesh,
        in_specs=placed,
        out_specs=(P(None, "ax", "xs", None, None), P(None, ("ax", "xs")), P(None, ("ax", "xs"))),
        check_vma=False,
    )
```

profile of v0, /device:TPU:1, one launch (start us, length us, event | category | flops | bytes accessed | tf_op | source)
XLA Modules:
  0.0 143.3 jit_solution(9744722386921598082)
XLA Ops:
  0.6 0.0 copy-start.3
  0.6 1.1 copy-done.3
  1.8 1.0 copy-done.4
  2.8 0.8 copy-done.7
  3.7 0.9 copy-done.9
  4.6 0.0 copy-start.8
  4.6 8.6 %shard_map.139 = (f32[3,512,256]{2,1,0:T(8,128)S(1)}, bf16[2048,256]{1,0:T(8,128)(2,1)S(1)}, f32[3,512,256]{2,1,0:T(8,128)}, f32[512,256]{1,0:T(8,128)S(1)}, f32...) custom-call(bf16[3,256,512]{2,1,0:T(8,128)(2,1)S(1)} %bitcast.44, ...), custom_call_target="tpu_custom_call" | custom-call | tf_op jit(solution)/shard_map/pallas_call | solution.py:344
  13.2 1.0 copy-done.1
  14.3 0.8 copy-done.5
  15.1 5.9 %collective-permute-start.4 = (f32[3,8,128]{2,1,0:T(8,128)S(1)}, f32[3,8,128]{2,1,0:T(8,128)S(1)}, u32[]{:S(2)}, u32[]{:S(2)}) collective-permute-start(f32[3,8,128]{2,1,0:T(8,128)S(1)} %get-tuple-element.43), channel_id=1, source_target_pairs={{0,17},{1,18},{2,19},{3,20},{4,21},{5,22},{6,23},{7,24},{8,25},{9,... | collective-permute-start | bytes 36872 | tf_op jit(solution)/shard_map/ppermute | solution.py:399
  21.0 1.9 %collective-permute-start.5 = (f32[3,8,128]{2,1,0:T(8,128)S(1)}, f32[3,8,128]{2,1,0:T(8,128)S(1)}, u32[]{:S(2)}, u32[]{:S(2)}) collective-permute-start(f32[3,8,128]{2,1,0:T(8,128)S(1)} %get-tuple-element.44), channel_id=1, source_target_pairs={{16,1},{17,2},{18,3},{19,4},{20,5},{21,6},{22,7},{23,8},{24,9},{25... | collective-permute-start | bytes 36872 | tf_op jit(solution)/shard_map/ppermute | solution.py:399
  22.9 7.9 %collective-permute-start.6 = (f32[3,8,128]{2,1,0:T(8,128)S(1)}, f32[3,8,128]{2,1,0:T(8,128)S(1)}, u32[]{:S(2)}, u32[]{:S(2)}) collective-permute-start(f32[3,8,128]{2,1,0:T(8,128)S(1)} %get-tuple-element.45), channel_id=1, source_target_pairs={{0,31},{1,16},{2,17},{3,18},{4,19},{5,20},{6,21},{7,22},{8,23},{9,... | collective-permute-start | bytes 36872 | tf_op jit(solution)/shard_map/ppermute | solution.py:399
  30.8 1.9 %collective-permute-start.7 = (f32[3,8,128]{2,1,0:T(8,128)S(1)}, f32[3,8,128]{2,1,0:T(8,128)S(1)}, u32[]{:S(2)}, u32[]{:S(2)}) collective-permute-start(f32[3,8,128]{2,1,0:T(8,128)S(1)} %get-tuple-element.46), channel_id=1, source_target_pairs={{16,15},{17,0},{18,1},{19,2},{20,3},{21,4},{22,5},{23,6},{24,7},{2... | collective-permute-start | bytes 36872 | tf_op jit(solution)/shard_map/ppermute | solution.py:399
  32.7 0.1 collective-permute-start.2
  32.9 3.1 %shard_map.142 = (f32[3,4096]{1,0:T(4,128)S(1)}, s32[1,4096]{1,0:T(1,128)S(1)}, f32[128,512]{1,0:T(8,128)S(1)}) custom-call(s32[3,4096]{1,0:T(4,128)S(1)} %copy-done.12, f32[3,4096]{1,0:T(4,128)S(1)} %copy-done.13, s32[1,4096]{1,0:T(1,128)S(1)} %bitcast.48, s32[1,4096]{1,0:T(1,128)S(1)} %bitcast.50), custom_call_target="tpu_custom_call" | custom-call | tf_op jit(solution)/shard_map/pallas_call | solution.py:344
  35.9 1.0 copy.33
  36.9 10.2 %all-to-all-start = ((f32[128,1,512]{2,1,0:T(1,128)}), f32[128,1,512]{2,1,0:T(1,128)}, u32[]{:S(2)}, u32[]{:S(2)}) async-start(f32[128,1,512]{2,1,0:T(1,128)} %copy.33), calls=%async_computation | async-start | bytes 524288 | tf_op jit(solution)/shard_map/all_to_all | solution.py:430
  47.1 0.0 collective-permute-done.4
  47.1 4.9 %collective-permute-start.3 = (f32[3,2,2,8,128]{4,3,2,1,0:T(8,128)S(1)}, f32[3,2,2,8,128]{4,3,2,1,0:T(8,128)S(1)}, u32[]{:S(2)}, u32[]{:S(2)}) collective-permute-start(f32[3,2,2,8,128]{4,3,2,1,0:T(8,128)S(1)} %get-tuple-element.27), channel_id=1, source_target_pairs={{0,15},{1,0},{2,1},{3,2},{4,3},{5,4},{6,5},{7,6},{8,7},{9,8},{10,9... | collective-permute-start | bytes 147464 | tf_op jit(solution)/shard_map/ppermute | solution.py:389
  52.0 0.0 collective-permute-done.5
  52.0 3.9 %collective-permute-start = (f32[3,64,128]{2,1,0:T(8,128)S(1)}, f32[3,64,128]{2,1,0:T(8,128)S(1)}, u32[]{:S(2)}, u32[]{:S(2)}) collective-permute-start(f32[3,64,128]{2,1,0:T(8,128)S(1)} %get-tuple-element.24), channel_id=1, source_target_pairs={{0,16},{16,32},{32,48},{48,64},{64,80},{80,96},{96,112},{1,17},{17... | collective-permute-start | bytes 294920 | tf_op jit(solution)/shard_map/ppermute | solution.py:392
  55.9 0.0 collective-permute-done.6
  55.9 1.9 %collective-permute-start.1 = (f32[3,64,128]{2,1,0:T(8,128)S(1)}, f32[3,64,128]{2,1,0:T(8,128)S(1)}, u32[]{:S(2)}, u32[]{:S(2)}) collective-permute-start(f32[3,64,128]{2,1,0:T(8,128)S(1)} %get-tuple-element.25), channel_id=1, source_target_pairs={{16,0},{32,16},{48,32},{64,48},{80,64},{96,80},{112,96},{17,1},{33... | collective-permute-start | bytes 294920 | tf_op jit(solution)/shard_map/ppermute | solution.py:392
  57.8 0.0 collective-permute-done.7
  57.9 0.0 collective-permute-done.2.left1
  57.9 0.0 collective-permute-done.3.right1
  57.9 0.0 collective-permute-done.low1
  57.9 4.0 %collective-permute-done.1.high1 = f32[3,64,128]{2,1,0:T(8,128)S(1)} collective-permute-done((f32[3,64,128]{2,1,0:T(8,128)S(1)}, f32[3,64,128]{2,1,0:T(8,128)S(1)}, u32[]{:S(2)}, u32[]{:S(2)}) %collective-permute-start.1) | collective-permute-done | bytes 98336 | tf_op jit(solution)/shard_map/ppermute | solution.py:392
  61.9 0.0 copy-done.8
  61.9 1.4 copy-done
  63.3 1.0 copy-done.6
  64.3 7.7 %shard_map.140 = (f32[3,512,256]{2,1,0:T(8,128)S(1)}, f32[3,64,128]{2,1,0:T(8,128)S(1)}, f32[3,64,128]{2,1,0:T(8,128)S(1)}, f32[3,2,2,8,128]{4,3,2,1,0:T(8,128)S(1)}, f32[3,2,2,8,128]{4,3,2,1,0:T(8,128)S(1)}) custom-call(f32[3,512,256]{2,1,0:T(8,128)S(1)} %get-tuple-element.21.h1, f32[3,512,256]{2,1,0:T(8,128)S(1)} %copy-done, f32[512,256]{1,0:T(8,128)S(1)} %copy-done.6, ...), custom_call_target="tpu_custom_call" | custom-call | tf_op jit(solution)/shard_map/pallas_call | solution.py:344
  72.0 0.0 copy-start.15
  72.0 0.6 copy-done.15
  72.7 1.9 %collective-permute-start.12 = (f32[3,8,128]{2,1,0:T(8,128)S(1)}, f32[3,8,128]{2,1,0:T(8,128)S(1)}, u32[]{:S(2)}, u32[]{:S(2)}) collective-permute-start(f32[3,8,128]{2,1,0:T(8,128)S(1)} %get-tuple-element.39), channel_id=1, source_target_pairs={{0,17},{1,18},{2,19},{3,20},{4,21},{5,22},{6,23},{7,24},{8,25},{9,... | collective-permute-start | bytes 36872 | tf_op jit(solution)/shard_map/ppermute | solution.py:399
  74.6 0.0 copy-start.17
  74.6 0.0 copy-start.18
  74.6 0.0 copy-start.16
  74.6 2.1 %collective-permute-start.13 = (f32[3,8,128]{2,1,0:T(8,128)S(1)}, f32[3,8,128]{2,1,0:T(8,128)S(1)}, u32[]{:S(2)}, u32[]{:S(2)}) collective-permute-start(f32[3,8,128]{2,1,0:T(8,128)S(1)} %get-tuple-element.40), channel_id=1, source_target_pairs={{16,1},{17,2},{18,3},{19,4},{20,5},{21,6},{22,7},{23,8},{24,9},{25... | collective-permute-start | bytes 36872 | tf_op jit(solution)/shard_map/ppermute | solution.py:399
  76.7 0.0 all-to-all-done
  76.7 1.0 copy.50
  77.7 1.2 copy-done.2
  78.9 20.9 %shard_map.143 = f32[128,512]{1,0:T(8,128)S(1)} custom-call(f32[128,512]{1,0:T(8,128)S(1)} %bitcast.42, bf16[2048,256]{1,0:T(8,128)(2,1)S(1)} %copy-done.2), custom_call_target="tpu_custom_call" | custom-call | tf_op jit(solution)/shard_map/pallas_call | solution.py:344
  99.8 1.0 copy.34
  100.8 10.1 %all-to-all-start.1 = ((f32[128,1,512]{2,1,0:T(1,128)}), f32[128,1,512]{2,1,0:T(1,128)S(1)}, u32[]{:S(2)}, u32[]{:S(2)}) async-start(f32[128,1,512]{2,1,0:T(1,128)} %copy.34), calls=%async_computation.1 | async-start | bytes 524288 | tf_op jit(solution)/shard_map/all_to_all | solution.py:443
  110.9 8.1 %collective-permute-start.14 = (f32[3,8,128]{2,1,0:T(8,128)S(1)}, f32[3,8,128]{2,1,0:T(8,128)S(1)}, u32[]{:S(2)}, u32[]{:S(2)}) collective-permute-start(f32[3,8,128]{2,1,0:T(8,128)S(1)} %get-tuple-element.41), channel_id=1, source_target_pairs={{0,31},{1,16},{2,17},{3,18},{4,19},{5,20},{6,21},{7,22},{8,23},{9,... | collective-permute-start | bytes 36872 | tf_op jit(solution)/shard_map/ppermute | solution.py:399
  119.1 1.9 %collective-permute-start.15 = (f32[3,8,128]{2,1,0:T(8,128)S(1)}, f32[3,8,128]{2,1,0:T(8,128)S(1)}, u32[]{:S(2)}, u32[]{:S(2)}) collective-permute-start(f32[3,8,128]{2,1,0:T(8,128)S(1)} %get-tuple-element.42), channel_id=1, source_target_pairs={{16,15},{17,0},{18,1},{19,2},{20,3},{21,4},{22,5},{23,6},{24,7},{2... | collective-permute-start | bytes 36872 | tf_op jit(solution)/shard_map/ppermute | solution.py:399
  121.0 0.1 copy.35.freq_ref
  121.1 0.1 copy.36.barrier_ref
  121.2 0.3 collective-permute-start.10
  121.5 0.0 collective-permute-done.12
  121.5 4.5 %collective-permute-start.11 = (f32[3,2,2,8,128]{4,3,2,1,0:T(8,128)S(1)}, f32[3,2,2,8,128]{4,3,2,1,0:T(8,128)S(1)}, u32[]{:S(2)}, u32[]{:S(2)}) collective-permute-start(f32[3,2,2,8,128]{4,3,2,1,0:T(8,128)S(1)} %get-tuple-element.32), channel_id=1, source_target_pairs={{0,15},{1,0},{2,1},{3,2},{4,3},{5,4},{6,5},{7,6},{8,7},{9,8},{10,9... | collective-permute-start | bytes 147464 | tf_op jit(solution)/shard_map/ppermute | solution.py:389
  126.0 0.0 collective-permute-done.13
  126.0 4.4 %collective-permute-start.8 = (f32[3,64,128]{2,1,0:T(8,128)S(1)}, f32[3,64,128]{2,1,0:T(8,128)S(1)}, u32[]{:S(2)}, u32[]{:S(2)}) collective-permute-start(f32[3,64,128]{2,1,0:T(8,128)S(1)} %copy-done.16), channel_id=1, source_target_pairs={{0,16},{16,32},{32,48},{48,64},{64,80},{80,96},{96,112},{1,17},{17... | collective-permute-start | bytes 294920 | tf_op jit(solution)/shard_map/ppermute | solution.py:392
  130.4 0.0 collective-permute-done.14
  130.4 1.9 %collective-permute-start.9 = (f32[3,64,128]{2,1,0:T(8,128)S(1)}, f32[3,64,128]{2,1,0:T(8,128)S(1)}, u32[]{:S(2)}, u32[]{:S(2)}) collective-permute-start(f32[3,64,128]{2,1,0:T(8,128)S(1)} %get-tuple-element.30), channel_id=1, source_target_pairs={{16,0},{32,16},{48,32},{64,48},{80,64},{96,80},{112,96},{17,1},{33... | collective-permute-start | bytes 294920 | tf_op jit(solution)/shard_map/ppermute | solution.py:392
  132.3 0.0 collective-permute-done.15
  132.4 0.0 collective-permute-done.10.left1
  132.4 0.0 collective-permute-done.11.right1
  132.4 0.0 collective-permute-done.8.low1
  132.4 4.0 %collective-permute-done.9.high1 = f32[3,64,128]{2,1,0:T(8,128)S(1)} collective-permute-done((f32[3,64,128]{2,1,0:T(8,128)S(1)}, f32[3,64,128]{2,1,0:T(8,128)S(1)}, u32[]{:S(2)}, u32[]{:S(2)}) %collective-permute-start.9) | collective-permute-done | bytes 98336 | tf_op jit(solution)/shard_map/ppermute | solution.py:392
  136.4 4.5 %shard_map.141 = f32[3,256,512]{2,1,0:T(8,128)} custom-call(f32[3,512,256]{2,1,0:T(8,128)S(1)} %get-tuple-element.28.h1, f32[3,64,128]{2,1,0:T(8,128)S(1)} %collective-permute-done.8.low1, f32[3,64,128]{2,1,0:T(8,128)S(1)} %collective-permute-done.9.high1, f32[3,2,2,8,128]{4,3,2,1,0:T(8,128)S(1)} %collective-permute-done.10.left1, ...), custom_call_target="tpu_custom_call" | custom-call | tf_op jit(solution)/shard_map/pallas_call | solution.py:344
  140.8 0.0 all-to-all-done.1
  140.8 2.5 %shard_map.144 = (f32[3,4096]{1,0:T(4,128)}, f32[6,4096]{1,0:T(8,128)}) custom-call(f32[128,512]{1,0:T(8,128)S(1)} %bitcast.41, s32[1,4096]{1,0:T(1,128)S(1)} %bitcast.49, s32[1,4096]{1,0:T(1,128)S(1)} %get-tuple-element.35.rank_ref, f32[3,4096]{1,0:T(4,128)S(1)} %get-tuple-element.36.coords_ref, f32[6,4096]{1,0:T(8,128)S(1)} %copy-done.10, ...), custom_call_target="tpu_custom_call" | custom-call | tf_op jit(solution)/shard_map/pallas_call | solution.py:344
  (28 shorter events, 0.1 us)
Async XLA Ops:
  0.6 1.1 copy-start.3
  1.8 1.0 copy-start.4
  2.8 0.8 copy-start.7
  3.6 0.9 copy-start.9
  4.6 28.2 %copy-start.11 = (s32[4096,1]{0,1:T(1,128)S(1)}, s32[4096,1]{0,1:T(1,128)}, u32[]{:S(2)}) copy-start(s32[4096,1]{0,1:T(1,128)} %param.18) | copy-start | bytes 49156
  4.6 28.2 %copy-start.12 = (s32[3,4096]{1,0:T(4,128)S(1)}, s32[3,4096]{1,0:T(4,128)}, u32[]{:S(2)}) copy-start(s32[3,4096]{1,0:T(4,128)} %idx_ref.1) | copy-start | bytes 147460
  4.6 28.2 %copy-start.13 = (f32[3,4096]{1,0:T(4,128)S(1)}, f32[3,4096]{1,0:T(4,128)}, u32[]{:S(2)}) copy-start(f32[3,4096]{1,0:T(4,128)} %off_ref.1) | copy-start | bytes 147460
  4.6 28.2 %copy-start.14 = (s32[4096]{0:T(1024)S(1)}, s32[4096]{0:T(1024)}, u32[]{:S(2)}) copy-start(s32[4096]{0:T(1024)} %param.19) | copy-start | bytes 49156
  4.6 57.2 %copy-start.8 = (f32[16,8,128]{2,1,0:T(8,128)S(1)}, f32[16,8,128]{2,1,0:T(8,128)}, u32[]{:S(2)}) copy-start(f32[16,8,128]{2,1,0:T(8,128)} %constant.2.clone.tables) | copy-start | bytes 196612
  13.2 1.0 copy-start.1
  14.3 0.8 copy-start.5
  15.1 32.1 %collective-permute-start.4 = (f32[3,8,128]{2,1,0:T(8,128)S(1)}, f32[3,8,128]{2,1,0:T(8,128)S(1)}, u32[]{:S(2)}, u32[]{:S(2)}) collective-permute-start(f32[3,8,128]{2,1,0:T(8,128)S(1)} %get-tuple-element.43), channel_id=1, source_target_pairs={{0,17},{1,18},{2,19},{3,20},{4,21},{5,22},{6,23},{7,24},{8,25},{9,... | collective-permute-start | bytes 36872 | tf_op jit(solution)/shard_map/ppermute | solution.py:399
  21.0 31.0 %collective-permute-start.5 = (f32[3,8,128]{2,1,0:T(8,128)S(1)}, f32[3,8,128]{2,1,0:T(8,128)S(1)}, u32[]{:S(2)}, u32[]{:S(2)}) collective-permute-start(f32[3,8,128]{2,1,0:T(8,128)S(1)} %get-tuple-element.44), channel_id=1, source_target_pairs={{16,1},{17,2},{18,3},{19,4},{20,5},{21,6},{22,7},{23,8},{24,9},{25... | collective-permute-start | bytes 36872 | tf_op jit(solution)/shard_map/ppermute | solution.py:399
  22.9 33.0 %collective-permute-start.6 = (f32[3,8,128]{2,1,0:T(8,128)S(1)}, f32[3,8,128]{2,1,0:T(8,128)S(1)}, u32[]{:S(2)}, u32[]{:S(2)}) collective-permute-start(f32[3,8,128]{2,1,0:T(8,128)S(1)} %get-tuple-element.45), channel_id=1, source_target_pairs={{0,31},{1,16},{2,17},{3,18},{4,19},{5,20},{6,21},{7,22},{8,23},{9,... | collective-permute-start | bytes 36872 | tf_op jit(solution)/shard_map/ppermute | solution.py:399
  30.8 27.0 %collective-permute-start.7 = (f32[3,8,128]{2,1,0:T(8,128)S(1)}, f32[3,8,128]{2,1,0:T(8,128)S(1)}, u32[]{:S(2)}, u32[]{:S(2)}) collective-permute-start(f32[3,8,128]{2,1,0:T(8,128)S(1)} %get-tuple-element.46), channel_id=1, source_target_pairs={{16,15},{17,0},{18,1},{19,2},{20,3},{21,4},{22,5},{23,6},{24,7},{2... | collective-permute-start | bytes 36872 | tf_op jit(solution)/shard_map/ppermute | solution.py:399
  32.7 25.1 %collective-permute-start.2 = (f32[3,2,2,8,128]{4,3,2,1,0:T(8,128)S(1)}, f32[3,2,2,8,128]{4,3,2,1,0:T(8,128)S(1)}, u32[]{:S(2)}, u32[]{:S(2)}) collective-permute-start(f32[3,2,2,8,128]{4,3,2,1,0:T(8,128)S(1)} %get-tuple-element.26), channel_id=1, source_target_pairs={{0,1},{1,2},{2,3},{3,4},{4,5},{5,6},{6,7},{7,8},{8,9},{9,10},{10,1... | collective-permute-start | bytes 147464 | tf_op jit(solution)/shard_map/ppermute | solution.py:389
  36.9 39.8 %all-to-all-start = ((f32[128,1,512]{2,1,0:T(1,128)}), f32[128,1,512]{2,1,0:T(1,128)}, u32[]{:S(2)}, u32[]{:S(2)}) async-start(f32[128,1,512]{2,1,0:T(1,128)} %copy.33), calls=%async_computation | async-start | bytes 524288 | tf_op jit(solution)/shard_map/all_to_all | solution.py:430
  47.1 10.7 %collective-permute-start.3 = (f32[3,2,2,8,128]{4,3,2,1,0:T(8,128)S(1)}, f32[3,2,2,8,128]{4,3,2,1,0:T(8,128)S(1)}, u32[]{:S(2)}, u32[]{:S(2)}) collective-permute-start(f32[3,2,2,8,128]{4,3,2,1,0:T(8,128)S(1)} %get-tuple-element.27), channel_id=1, source_target_pairs={{0,15},{1,0},{2,1},{3,2},{4,3},{5,4},{6,5},{7,6},{8,7},{9,8},{10,9... | collective-permute-start | bytes 147464 | tf_op jit(solution)/shard_map/ppermute | solution.py:389
  52.0 5.9 %collective-permute-start = (f32[3,64,128]{2,1,0:T(8,128)S(1)}, f32[3,64,128]{2,1,0:T(8,128)S(1)}, u32[]{:S(2)}, u32[]{:S(2)}) collective-permute-start(f32[3,64,128]{2,1,0:T(8,128)S(1)} %get-tuple-element.24), channel_id=1, source_target_pairs={{0,16},{16,32},{32,48},{48,64},{64,80},{80,96},{96,112},{1,17},{17... | collective-permute-start | bytes 294920 | tf_op jit(solution)/shard_map/ppermute | solution.py:392
  55.9 5.9 %collective-permute-start.1 = (f32[3,64,128]{2,1,0:T(8,128)S(1)}, f32[3,64,128]{2,1,0:T(8,128)S(1)}, u32[]{:S(2)}, u32[]{:S(2)}) collective-permute-start(f32[3,64,128]{2,1,0:T(8,128)S(1)} %get-tuple-element.25), channel_id=1, source_target_pairs={{16,0},{32,16},{48,32},{64,48},{80,64},{96,80},{112,96},{17,1},{33... | collective-permute-start | bytes 294920 | tf_op jit(solution)/shard_map/ppermute | solution.py:392
  61.9 1.4 copy-start
  63.3 1.0 copy-start.6
  72.0 0.6 copy-start.15
  72.7 48.8 %collective-permute-start.12 = (f32[3,8,128]{2,1,0:T(8,128)S(1)}, f32[3,8,128]{2,1,0:T(8,128)S(1)}, u32[]{:S(2)}, u32[]{:S(2)}) collective-permute-start(f32[3,8,128]{2,1,0:T(8,128)S(1)} %get-tuple-element.39), channel_id=1, source_target_pairs={{0,17},{1,18},{2,19},{3,20},{4,21},{5,22},{6,23},{7,24},{8,25},{9,... | collective-permute-start | bytes 36872 | tf_op jit(solution)/shard_map/ppermute | solution.py:399
  74.6 46.4 %copy-start.17 = (f32[6]{0:T(128)S(1)}, f32[6]{0:T(128)}, u32[]{:S(2)}) copy-start(f32[6]{0:T(128)} %param.21) | copy-start | bytes 76
  74.6 46.5 %copy-start.18 = (f32[6]{0:T(128)S(1)}, f32[6]{0:T(128)}, u32[]{:S(2)}) copy-start(f32[6]{0:T(128)} %param.22) | copy-start | bytes 76
  74.6 51.4 %copy-start.16 = (f32[3,64,128]{2,1,0:T(8,128)S(1)}, f32[3,64,128]{2,1,0:T(8,128)}, u32[]{:S(2)}) copy-start(f32[3,64,128]{2,1,0:T(8,128)} %copy-done.15) | copy-start | bytes 294916
  74.6 51.4 %collective-permute-start.13 = (f32[3,8,128]{2,1,0:T(8,128)S(1)}, f32[3,8,128]{2,1,0:T(8,128)S(1)}, u32[]{:S(2)}, u32[]{:S(2)}) collective-permute-start(f32[3,8,128]{2,1,0:T(8,128)S(1)} %get-tuple-element.40), channel_id=1, source_target_pairs={{16,1},{17,2},{18,3},{19,4},{20,5},{21,6},{22,7},{23,8},{24,9},{25... | collective-permute-start | bytes 36872 | tf_op jit(solution)/shard_map/ppermute | solution.py:399
  77.7 1.2 copy-start.2
  100.8 40.0 %all-to-all-start.1 = ((f32[128,1,512]{2,1,0:T(1,128)}), f32[128,1,512]{2,1,0:T(1,128)S(1)}, u32[]{:S(2)}, u32[]{:S(2)}) async-start(f32[128,1,512]{2,1,0:T(1,128)} %copy.34), calls=%async_computation.1 | async-start | bytes 524288 | tf_op jit(solution)/shard_map/all_to_all | solution.py:443
  110.9 19.5 %collective-permute-start.14 = (f32[3,8,128]{2,1,0:T(8,128)S(1)}, f32[3,8,128]{2,1,0:T(8,128)S(1)}, u32[]{:S(2)}, u32[]{:S(2)}) collective-permute-start(f32[3,8,128]{2,1,0:T(8,128)S(1)} %get-tuple-element.41), channel_id=1, source_target_pairs={{0,31},{1,16},{2,17},{3,18},{4,19},{5,20},{6,21},{7,22},{8,23},{9,... | collective-permute-start | bytes 36872 | tf_op jit(solution)/shard_map/ppermute | solution.py:399
  119.1 13.3 %collective-permute-start.15 = (f32[3,8,128]{2,1,0:T(8,128)S(1)}, f32[3,8,128]{2,1,0:T(8,128)S(1)}, u32[]{:S(2)}, u32[]{:S(2)}) collective-permute-start(f32[3,8,128]{2,1,0:T(8,128)S(1)} %get-tuple-element.42), channel_id=1, source_target_pairs={{16,15},{17,0},{18,1},{19,2},{20,3},{21,4},{22,5},{23,6},{24,7},{2... | collective-permute-start | bytes 36872 | tf_op jit(solution)/shard_map/ppermute | solution.py:399
  121.2 11.2 %collective-permute-start.10 = (f32[3,2,2,8,128]{4,3,2,1,0:T(8,128)S(1)}, f32[3,2,2,8,128]{4,3,2,1,0:T(8,128)S(1)}, u32[]{:S(2)}, u32[]{:S(2)}) collective-permute-start(f32[3,2,2,8,128]{4,3,2,1,0:T(8,128)S(1)} %get-tuple-element.31), channel_id=1, source_target_pairs={{0,1},{1,2},{2,3},{3,4},{4,5},{5,6},{6,7},{7,8},{8,9},{9,10},{10,1... | collective-permute-start | bytes 147464 | tf_op jit(solution)/shard_map/ppermute | solution.py:389
  121.5 10.9 %collective-permute-start.11 = (f32[3,2,2,8,128]{4,3,2,1,0:T(8,128)S(1)}, f32[3,2,2,8,128]{4,3,2,1,0:T(8,128)S(1)}, u32[]{:S(2)}, u32[]{:S(2)}) collective-permute-start(f32[3,2,2,8,128]{4,3,2,1,0:T(8,128)S(1)} %get-tuple-element.32), channel_id=1, source_target_pairs={{0,15},{1,0},{2,1},{3,2},{4,3},{5,4},{6,5},{7,6},{8,7},{9,8},{10,9... | collective-permute-start | bytes 147464 | tf_op jit(solution)/shard_map/ppermute | solution.py:389
  126.0 6.4 %collective-permute-start.8 = (f32[3,64,128]{2,1,0:T(8,128)S(1)}, f32[3,64,128]{2,1,0:T(8,128)S(1)}, u32[]{:S(2)}, u32[]{:S(2)}) collective-permute-start(f32[3,64,128]{2,1,0:T(8,128)S(1)} %copy-done.16), channel_id=1, source_target_pairs={{0,16},{16,32},{32,48},{48,64},{64,80},{80,96},{96,112},{1,17},{17... | collective-permute-start | bytes 294920 | tf_op jit(solution)/shard_map/ppermute | solution.py:392
  130.4 5.9 %collective-permute-start.9 = (f32[3,64,128]{2,1,0:T(8,128)S(1)}, f32[3,64,128]{2,1,0:T(8,128)S(1)}, u32[]{:S(2)}, u32[]{:S(2)}) collective-permute-start(f32[3,64,128]{2,1,0:T(8,128)S(1)} %get-tuple-element.30), channel_id=1, source_target_pairs={{16,0},{32,16},{48,32},{64,48},{80,64},{96,80},{112,96},{17,1},{33... | collective-permute-start | bytes 294920 | tf_op jit(solution)/shard_map/ppermute | solution.py:392
  136.4 4.5 %copy-start.10 = (f32[6,4096]{1,0:T(8,128)S(1)}, f32[6,4096]{1,0:T(8,128)}, u32[]{:S(2)}) copy-start(f32[6,4096]{1,0:T(8,128)} %share_ref.1) | copy-start | bytes 294916
where the time goes:
time: 144 us; the launch traced here: 143 us
  starting transfers between devices  73.9 us (51%)
  Pallas kernels  47.2 us (33%)
  local copies, waits for them, and re-layouts  13.3 us (9%)
  waiting for transfers between devices  7.94 us (6%)
    pallas_call x6, Pallas kernels, call(): pl.pallas_call(body, out_shape=[jax.ShapeDtypeStruct(shape, dtype) for sh...  47.2 us
    ppermute x8, starting transfers between devices, shift(): return lax.ppermute(value, ('ax', 'xs'), pairs)  31.7 us
    ppermute x4, starting transfers between devices, shift(): return lax.ppermute(value, 'ax', pairs)  12.1 us
    unnamed x40, local copies, waits for them, and re-layouts  11.1 us
    all_to_all x1, starting transfers between devices, local(): lax.all_to_all(payload, ('ax', 'xs'), split_axis=0, concat_axis=0, tiled=...  10.2 us
    all_to_all x1, starting transfers between devices, local(): lax.all_to_all(values, ('ax', 'xs'), split_axis=0, concat_axis=0, tiled=T...  10.1 us
    ppermute x4, starting transfers between devices, shift(): return lax.ppermute(value, 'xs', pairs)  9.74 us
    ppermute x4, waiting for transfers between devices, shift(): return lax.ppermute(value, 'ax', pairs)  7.91 us
  transfers between devices with their start and end apart: 18, of which 2 were waited for; matrix products, arithmetic and copies ran while one was open for 2% of the time, Pallas kernels for 25%

commit v1 on v0

v1 whole, which is shorter than its diff:
```python
import functools

import jax
import jax.numpy as jnp
import numpy as np
from jax import lax
from jax.experimental import pallas as pl
from jax.experimental.pallas import tpu as pltpu
from jax.sharding import PartitionSpec as P

NODE_LIST = (
    -1.0,
    -0.8717401485096066,
    -0.5917001814331423,
    -0.2092992179024789,
    0.2092992179024789,
    0.5917001814331423,
    0.8717401485096066,
    1.0,
)
STEP_DT = 0.25
F32 = jnp.float32
BF16 = jnp.bfloat16
CHUNK = 256


def bary_weights():
    nodes = np.array(NODE_LIST)
    weights = np.zeros(8)
    for a in range(8):
        weights[a] = 1.0 / np.prod([nodes[a] - nodes[m] for m in range(8) if m != a])
    return nodes, weights


def deriv_table():
    nodes, weights = bary_weights()
    table = np.zeros((8, 8))
    for row in range(8):
        for col in range(8):
            if row != col:
                table[row, col] = weights[col] / weights[row] / (nodes[row] - nodes[col])
        table[row, row] = -np.sum(table[row])
    return table


DM = np.asarray(deriv_table(), np.float32).astype(np.float64)


def fill_tables(t_ref):
    sub = lax.broadcasted_iota(jnp.int32, (8, 128), 0)
    for half, table in enumerate((DM, DM.T)):
        for s in range(8):
            out = jnp.full((8, 128), table[0, (0 - s) % 8], F32)
            for p in range(1, 8):
                out = jnp.where(sub == p, F32(table[p, (p - s) % 8]), out)
            t_ref[half * 8 + s] = out


def apply_table(table, u):
    even = [u[i] + u[7 - i] for i in range(4)]
    odd = [u[i] - u[7 - i] for i in range(4)]
    out = [None] * 8
    for p in range(4):
        a = b = None
        for i in range(4):
            ca = float((table[p, i] + table[p, 7 - i]) / 2)
            cb = float((table[p, i] - table[p, 7 - i]) / 2)
            ta, tb = even[i] * ca, odd[i] * cb
            a = ta if a is None else a + ta
            b = tb if b is None else b + tb
        out[p], out[7 - p] = a + b, b - a
    return out


def apply_rolls(tables, x):
    y = x * tables[0]
    for s in range(1, 8):
        y = y + pltpu.roll(x, s, 0) * tables[s]
    return y


def pick_node(cell, shift):
    out = jnp.full(cell.shape, NODE_LIST[shift], F32)
    for c in range(1, 7):
        out = jnp.where(cell == c, F32(NODE_LIST[c + shift]), out)
    return out


def split(x):
    high = x.astype(BF16).astype(F32)
    return high, x - high


def dispatch(idx_ref, off_ref, own_ref, piece_ref, coords_ref, rank_ref, pay_ref):
    total = idx_ref.shape[1]
    cell = idx_ref[...]
    low, high = pick_node(cell, 0), pick_node(cell, 1)
    coords_ref[...] = low + off_ref[...] * (high - low)
    rows = lax.broadcasted_iota(jnp.int32, (CHUNK, 2 * CHUNK), 0)
    cols = lax.broadcasted_iota(jnp.int32, (CHUNK, 2 * CHUNK), 1)
    before = jnp.where((rows < cols) | (cols >= CHUNK), 1.0, 0.0).astype(BF16)
    lane_id = lax.broadcasted_iota(jnp.int32, (128, CHUNK), 0)
    base = jnp.zeros((128, CHUNK), F32)
    for c in range(total // CHUNK):
        part = pl.ds(c * CHUNK, CHUNK)
        hot = jnp.where(own_ref[:, part] == lane_id, 1.0, 0.0)
        count = jnp.dot(hot.astype(BF16), before, preferred_element_type=F32)
        rank = jnp.sum(hot * (count[:, :CHUNK] + base), axis=0, keepdims=True)
        rank_ref[:, part] = rank.astype(jnp.int32)
        base = base + count[:, CHUNK:]
    sums = [jnp.zeros((128, 128), F32)] * 4
    dims = (((1,), (1,)), ((), ()))
    for c in range(total // CHUNK):
        part = pl.ds(c * CHUNK, CHUNK)
        hot = jnp.where(own_ref[:, part] == lane_id, 1.0, 0.0).astype(BF16)
        mask = rank_ref[:, part] == lane_id
        tops, lows = [], []
        for d in range(3):
            high, rest = split(coords_ref[pl.ds(d, 1), part])
            tops.append(jnp.where(mask, high, 0.0).astype(BF16))
            lows.append(jnp.where(mask, rest, 0.0).astype(BF16))
        tops.append(jnp.where(mask, piece_ref[:, part].astype(F32), 0.0).astype(BF16))
        one = lax.dot_general(hot, jnp.concatenate(tops, 0), dims, preferred_element_type=F32)
        two = lax.dot_general(hot, jnp.concatenate(lows, 0), dims, preferred_element_type=F32)
        sums = [
            sums[v] + (one[:, v * 128 : (v + 1) * 128] + two[:, v * 128 : (v + 1) * 128] if v < 3 else one[:, 384:])
            for v in range(4)
        ]
    for v in range(4):
        pay_ref[:, v, :] = sums[v]


def interpolate(base, got_ref, table_ref, back_ref, lag_ref):
    nodes, weights = bary_weights()
    ident = lax.broadcasted_iota(jnp.int32, (256, 256), 0)
    for d in range(3):
        x = got_ref[pl.ds(base, 8), d, :]
        diff = [x - F32(n) for n in nodes]
        ahead, behind = [None] * 8, [None] * 8
        ahead[1], behind[6] = diff[0], diff[7]
        for i in range(2, 8):
            ahead[i] = ahead[i - 1] * diff[i - 1]
            behind[7 - i] = behind[8 - i] * diff[8 - i]
        for i in range(8):
            prod = behind[0] if i == 0 else ahead[7] if i == 7 else ahead[i] * behind[i]
            lag_ref[pl.ds(d * 64 + i * 8, 8), :] = prod * F32(weights[i])
    elem = got_ref[pl.ds(base, 8), 3, :].astype(jnp.int32)
    for pair in range(4):
        s0, s1 = 2 * pair, 2 * pair + 1
        ids = jnp.concatenate([elem[s0 : s0 + 1], elem[s1 : s1 + 1]], 1)
        hot = jnp.where(ident == ids, 1.0, 0.0).astype(BF16)

        def weight(d, i):
            row = d * 64 + i * 8
            return jnp.concatenate(
                [lag_ref[pl.ds(row + s0, 1), :], lag_ref[pl.ds(row + s1, 1), :]], 1
            )

        third = jnp.concatenate(
            [lag_ref[pl.ds(128 + s0, 8, stride=8), :], lag_ref[pl.ds(128 + s1, 8, stride=8), :]], 1
        )
        for f in range(4):
            rows = jnp.dot(table_ref[pl.ds(f * 512, 512), :], hot, preferred_element_type=F32)
            one = None
            for i in range(8):
                term = rows[i * 64 : (i + 1) * 64] * weight(0, i)
                one = term if one is None else one + term
            two = None
            for j in range(8):
                term = one[j * 8 : (j + 1) * 8] * weight(1, j)
                two = term if two is None else two + term
            value = jnp.sum(two * third, axis=0, keepdims=True)
            back_ref[base + s0, pl.ds(f, 1), :] = value[:, :128]
            back_ref[base + s1, pl.ds(f, 1), :] = value[:, 128:]


def gather_back(ret_ref, own_ref, rank_ref, probe_ref, halves_ref):
    total = own_ref.shape[1]
    for f in range(4):
        high, rest = split(jnp.transpose(ret_ref[:, f, :]))
        halves_ref[pl.ds(f * 128, 128), 0:128] = high.astype(BF16)
        halves_ref[pl.ds(f * 128, 128), 128:256] = rest.astype(BF16)
    lane_id = lax.broadcasted_iota(jnp.int32, (128, CHUNK), 0)
    for c in range(total // CHUNK):
        part = pl.ds(c * CHUNK, CHUNK)
        hot = jnp.where(own_ref[:, part] == lane_id, 1.0, 0.0).astype(BF16)
        found = jnp.dot(
            halves_ref[...], jnp.concatenate([hot, hot], 0), preferred_element_type=F32
        )
        mask = rank_ref[:, part] == lane_id
        for f in range(4):
            kept = jnp.where(mask, found[f * 128 : (f + 1) * 128], 0.0)
            probe_ref[pl.ds(f, 1), part] = jnp.sum(kept, axis=0, keepdims=True)


def kinetics(probe_ref, coords_ref, share_ref, freq_ref, barrier_ref, cnew_ref, snew_ref):
    cnew_ref[...] = coords_ref[...] + STEP_DT * probe_ref[0:3, :]
    rates = freq_ref[...] * jnp.exp(barrier_ref[...] * jnp.tanh(probe_ref[3:4, :] - 1.0))
    shares = share_ref[...]
    flux = rates * shares
    moved = jnp.concatenate([flux[5:6], flux[0:5]], 0)
    snew_ref[...] = shares + STEP_DT * (moved - flux)


def turn_in(flow_ref, heat_ref, stiff_ref, inert_ref, x_ref, table_ref, g_ref, c_ref):
    def three(d, carry):
        for a in range(2):
            lanes = pl.ds(a * 128, 128)
            turned = jnp.transpose(flow_ref[d, lanes, :].astype(F32))
            x_ref[d, :, lanes] = turned
            table_ref[pl.ds(pl.multiple_of(d * 512, 512), 512), lanes] = turned.astype(BF16)
            g_ref[d, :, lanes] = jnp.transpose(stiff_ref[d, lanes, :])
        return carry

    lax.fori_loop(0, 3, three, 0)
    for a in range(2):
        lanes = pl.ds(a * 128, 128)
        table_ref[pl.ds(1536, 512), lanes] = jnp.transpose(heat_ref[lanes, :].astype(F32)).astype(BF16)
        c_ref[:, lanes] = jnp.transpose(inert_ref[lanes, :])


def helm(x_ref, g_ref, c_ref, t_ref, h_ref):
    def part(n, carry):
        f, a = n // 2, n % 2
        lanes = pl.ds(pl.multiple_of(a * 128, 128), 128)
        fore = [t_ref[s] for s in range(8)]
        aft = [t_ref[8 + s] for s in range(8)]
        for i in range(8):
            at = [pl.ds(i * 64 + j * 8, 8) for j in range(8)]
            x = [x_ref[f, at[j], lanes] for j in range(8)]
            dj = apply_table(DM, x)
            dj = [g_ref[1, at[j], lanes] * dj[j] for j in range(8)]
            dj = apply_table(DM.T, dj)
            for j in range(8):
                dk = g_ref[2, at[j], lanes] * apply_rolls(fore, x[j])
                h_ref[f, at[j], lanes] = dj[j] + c_ref[at[j], lanes] * x[j] + apply_rolls(aft, dk)
        for j in range(8):
            at = [pl.ds(i * 64 + j * 8, 8) for i in range(8)]
            di = apply_table(DM, [x_ref[f, at[i], lanes] for i in range(8)])
            di = [g_ref[0, at[i], lanes] * di[i] for i in range(8)]
            di = apply_table(DM.T, di)
            for i in range(8):
                h_ref[f, at[i], lanes] += di[i]
        return carry

    lax.fori_loop(0, 6, part, 0)


def faces(h_ref, low_ref, high_ref, left_ref, right_ref):
    for f in range(3):
        low_ref[f] = h_ref[f, 0:64, 0:128]
        high_ref[f] = h_ref[f, 448:512, 128:256]
        both = h_ref[f, 448:512, 0:128] + h_ref[f, 0:64, 128:256]
        h_ref[f, 448:512, 0:128] = both
        h_ref[f, 0:64, 128:256] = both
    lane = lax.broadcasted_iota(jnp.int32, (8, 128), 1) // 32

    def pack(n, carry):
        f, a = n // 2, n % 2
        lanes = pl.ds(pl.multiple_of(a * 128, 128), 128)
        for half in range(2):
            one = two = None
            for q in range(4):
                row = (half * 4 + q) * 64
                first = h_ref[f, pl.ds(row, 8), lanes]
                last = h_ref[f, pl.ds(row + 56, 8), lanes]
                if q:
                    first = pltpu.roll(first, 32 * q, 1)
                if q < 3:
                    last = pltpu.roll(last, 32 * q + 32, 1)
                one = first if one is None else jnp.where(lane == q, first, one)
                two = last if two is None else jnp.where(lane == q, last, two)
            left_ref[f, a, half] = one
            right_ref[f, a, half] = two
        return carry

    lax.fori_loop(0, 6, pack, 0)


def assemble(h_ref, x_ref, low_ref, high_ref, left_ref, right_ref, corner_ref, lowest, highest):
    lane = lax.broadcasted_iota(jnp.int32, (8, 128), 1)
    sub = lax.broadcasted_iota(jnp.int32, (8, 128), 0)
    quarter, radial = lane // 32, lane % 32
    at_first = (sub == 0) & (radial != 0)
    at_last = (sub == 7) & (radial != 31)

    under = jnp.where(lowest, F32(0.0), F32(1.0))
    over = jnp.where(highest, F32(0.0), F32(1.0))

    def near(f, carry):
        def corner(n, q, turn, scale):
            return jnp.where(quarter == q, pltpu.roll(corner_ref[n, f], turn, 1) * scale, 0.0)

        h_ref[f, 0:64, 0:128] += low_ref[f] * under
        h_ref[f, 448:512, 128:256] += high_ref[f] * over
        left_ref[f, 0, 0] += corner(0, 0, 32, under)
        left_ref[f, 1, 1] += corner(1, 3, 96, over)
        right_ref[f, 0, 0] += corner(2, 0, 32, under)
        right_ref[f, 1, 1] += corner(3, 3, 96, over)
        return carry

    lax.fori_loop(0, 3, near, 0)

    def radially(x):
        up = pltpu.roll(pltpu.roll(x, 1, 1), 1, 0)
        down = pltpu.roll(pltpu.roll(x, 127, 1), 7, 0)
        return x + jnp.where(at_first, up, 0.0) + jnp.where(at_last, down, 0.0)

    def part(n, carry):
        f, a = n // 2, n % 2
        lanes = pl.ds(pl.multiple_of(a * 128, 128), 128)
        for i in range(8):
            half, q = i // 4, i % 4
            first = h_ref[f, pl.ds(i * 64, 8), lanes]
            last = h_ref[f, pl.ds(i * 64 + 56, 8), lanes]
            before, after = left_ref[f, a, half], right_ref[f, a, half]
            if q:
                before = pltpu.roll(before, 128 - 32 * q, 1)
            if q < 3:
                after = pltpu.roll(after, 96 - 32 * q, 1)
            before = jnp.where(quarter == 0, before, pltpu.roll(last, 32, 1))
            after = jnp.where(quarter == 3, after, pltpu.roll(first, 96, 1))
            x_ref[f, pl.ds(i * 64, 8), lanes] = radially(first + before)
            x_ref[f, pl.ds(i * 64 + 56, 8), lanes] = radially(last + after)
            for j in range(1, 7):
                row = pl.ds(i * 64 + j * 8, 8)
                x_ref[f, row, lanes] = radially(h_ref[f, row, lanes])
        return carry

    lax.fori_loop(0, 6, part, 0)


FIELD = ((3, 512, 256), F32)
FACE = ((3, 64, 128), F32)
SIDE = ((3, 2, 2, 8, 128), F32)
CORNER = ((4, 3, 8, 128), F32)
RIMS = [FACE, FACE, SIDE, SIDE]
SLOTS = ((128, 4, 128), F32)
MESH = pl.DeviceIdType.MESH
LIMIT = 56 * 1024 * 1024


def rim_copies(n_ax, n_xs, sent, landed, corners, send_sems, recv_sems):
    ax, xs = lax.axis_index("ax"), lax.axis_index("xs")
    low, high, left, right = sent
    plan = [
        (high, landed[0], 1, 0),
        (low, landed[1], -1, 0),
        (right, landed[2], 0, 1),
        (left, landed[3], 0, -1),
        (right.at[:, 1, 1], corners.at[0], 1, 1),
        (right.at[:, 0, 0], corners.at[1], -1, 1),
        (left.at[:, 1, 1], corners.at[2], 1, -1),
        (left.at[:, 0, 0], corners.at[3], -1, -1),
    ]
    return [
        pltpu.make_async_remote_copy(
            src_ref=src,
            dst_ref=dst,
            send_sem=send_sems.at[n],
            recv_sem=recv_sems.at[n],
            device_id=(lax.rem(ax + da + n_ax, n_ax), lax.rem(xs + dx + n_xs, n_xs)),
            device_id_type=MESH,
        )
        for n, (src, dst, da, dx) in enumerate(plan)
    ]


def main_body(n_ax, n_xs, *refs):
    (flow_h, heat_h, stiff_h, inert_h, idx_h, off_h, own_h, piece_h) = refs[:8]
    (h2, low4, high4, left4, right4, corners2, probe, coords) = refs[8:16]
    (flow, heat, stiff, inert, idx, off, own, piece) = refs[16:24]
    (rank, pay, got, back, ret, x, h, g, c, table, tables, lag, halves) = refs[24:37]
    (low1, high1, left1, right1, low2, high2, left2, right2, corners1) = refs[37:46]
    (low3, high3, left3, right3) = refs[46:50]
    (in_sems, out_send, out_recv, back_send, back_recv, rim_send, rim_recv) = refs[50:]
    devices = n_ax * n_xs
    ax, xs = lax.axis_index("ax"), lax.axis_index("xs")
    me = ax * n_xs + xs

    loads = [
        pltpu.make_async_copy(src, dst, in_sems.at[n])
        for n, (src, dst) in enumerate(
            zip(
                (idx_h, off_h, own_h, piece_h, flow_h, heat_h, stiff_h, inert_h),
                (idx, off, own, piece, flow, heat, stiff, inert),
            )
        )
    ]
    for load in loads:
        load.start()

    def where(n):
        return (lax.div(n, n_xs), lax.rem(n, n_xs))

    barrier = pltpu.get_barrier_semaphore()

    def greet(k, carry):
        pl.semaphore_signal(
            barrier, inc=1, device_id=where(lax.rem(me + k, devices)), device_id_type=MESH
        )
        return carry

    lax.fori_loop(1, devices, greet, 0)
    fill_tables(tables)
    for load in loads[:4]:
        load.wait()
    dispatch(idx, off, own, piece, coords, rank, pay)
    pl.semaphore_wait(barrier, devices - 1)

    group = lax.div(me, 8)
    own_copy = pltpu.make_async_copy(pay.at[me], got.at[me], out_recv.at[group])
    own_copy.start()

    def send(k, carry):
        to = lax.rem(me + k, devices)
        pltpu.make_async_remote_copy(
            src_ref=pay.at[to],
            dst_ref=got.at[me],
            send_sem=out_send,
            recv_sem=out_recv.at[group],
            device_id=where(to),
            device_id_type=MESH,
        ).start()
        return carry

    lax.fori_loop(1, devices, send, 0)

    for load in loads[4:]:
        load.wait()
    turn_in(flow, heat, stiff, inert, x, table, g, c)
    helm(x, g, c, tables, h)
    faces(h, low1, high1, left1, right1)
    first = rim_copies(
        n_ax, n_xs, (low1, high1, left1, right1), (low2, high2, left2, right2), corners1,
        rim_send.at[0], rim_recv.at[0],
    )
    for copy in first:
        copy.start()

    def block(n, carry):
        now = lax.rem(group + 2 * (devices // 8) - 1 - n, devices // 8)
        base = now * 8
        rows = got.at[pl.ds(base, 8)]
        pltpu.make_async_copy(rows, rows, out_recv.at[now]).wait()
        interpolate(base, got, table, back, lag)

        def give(s, inner):
            to = base + s

            @pl.when(to != me)
            def _():
                pltpu.make_async_remote_copy(
                    src_ref=back.at[to],
                    dst_ref=ret.at[me],
                    send_sem=back_send,
                    recv_sem=back_recv,
                    device_id=where(to),
                    device_id_type=MESH,
                ).start()

            @pl.when(to == me)
            def _():
                pltpu.make_async_copy(back.at[to], ret.at[me], back_recv).start()

            return inner

        lax.fori_loop(0, 8, give, 0)
        return carry

    lax.fori_loop(0, devices // 8, block, 0)

    for copy in first:
        copy.wait()
    assemble(h, x, low2, high2, left2, right2, corners1, ax == 0, ax == n_ax - 1)
    helm(x, g, c, tables, h2)
    faces(h2, low3, high3, left3, right3)
    second = rim_copies(
        n_ax, n_xs, (low3, high3, left3, right3), (low4, high4, left4, right4), corners2,
        rim_send.at[1], rim_recv.at[1],
    )
    for copy in second:
        copy.start()

    pltpu.make_async_copy(ret, ret, back_recv).wait()
    gather_back(ret, own, rank, probe, halves)

    others = pl.ds(0, devices - 1)
    pltpu.make_async_copy(pay.at[others], pay.at[others], out_send).wait()
    pltpu.make_async_copy(back.at[others], back.at[others], back_send).wait()
    for copy in second:
        copy.wait()


def last_body(h1, low1, high1, left1, right1, corners, probe, coords, shares, freq, barrier, out, cnew, snew, x, work, l1, r1, turned, sems):
    ax, n_ax = lax.axis_index("ax"), lax.axis_size("ax")
    kinetics(probe, coords, shares, freq, barrier, cnew, snew)
    work[...] = h1[...]
    l1[...] = left1[...]
    r1[...] = right1[...]
    assemble(work, x, low1, high1, l1, r1, corners, ax == 0, ax == n_ax - 1)
    copies = []
    for d in range(3):
        for a in range(2):
            lanes = pl.ds(a * 128, 128)
            turned[d, lanes, :] = jnp.transpose(x[d, :, lanes])
            copy = pltpu.make_async_copy(turned.at[d, lanes], out.at[d, lanes], sems.at[d * 2 + a])
            copy.start()
            copies.append(copy)
    for copy in copies:
        copy.wait()


def shapes(outs):
    return [jax.ShapeDtypeStruct(shape, dtype) for shape, dtype in outs]


def buffers(outs):
    return [pltpu.VMEM(shape, dtype) for shape, dtype in outs]


def local(flow, heat, stiff, inert, index, offset, owner, piece, shares, freq, barrier):
    particles = piece.shape[0]
    n_ax, n_xs = lax.axis_size("ax"), lax.axis_size("xs")
    devices = n_ax * n_xs
    vmem = pl.BlockSpec(memory_space=pltpu.VMEM)
    hbm = pl.BlockSpec(memory_space=pltpu.HBM)
    inputs = (
        flow.reshape(3, 256, 512),
        heat.reshape(256, 512),
        stiff.reshape(3, 256, 512),
        inert.reshape(256, 512),
        index,
        offset,
        owner.reshape(1, particles),
        piece.reshape(1, particles),
    )
    held = [(a.shape, a.dtype) for a in inputs]
    table = ((2048, 256), BF16)
    outs = [FIELD, *RIMS, CORNER, ((4, particles), F32), ((3, particles), F32)]
    passed = pl.pallas_call(
        functools.partial(main_body, n_ax, n_xs),
        out_shape=shapes(outs),
        in_specs=[hbm] * 8,
        out_specs=[vmem] * len(outs),
        scratch_shapes=buffers(held)
        + buffers([((1, particles), jnp.int32), SLOTS, SLOTS, SLOTS, SLOTS, FIELD, FIELD, FIELD])
        + buffers([((512, 256), F32), table, ((16, 8, 128), F32), ((192, 128), F32), ((512, 256), BF16)])
        + buffers([*RIMS, *RIMS, CORNER, *RIMS])
        + [
            pltpu.SemaphoreType.DMA((8,)),
            pltpu.SemaphoreType.DMA,
            pltpu.SemaphoreType.DMA((devices // 8,)),
            pltpu.SemaphoreType.DMA,
            pltpu.SemaphoreType.DMA,
            pltpu.SemaphoreType.DMA((2, 8)),
            pltpu.SemaphoreType.DMA((2, 8)),
        ],
        compiler_params=pltpu.CompilerParams(
            collective_id=0, has_side_effects=True, vmem_limit_bytes=LIMIT
        ),
    )(*inputs)
    outs = [((3, 256, 512), F32), ((3, particles), F32), ((6, particles), F32)]
    out, cnew, snew = pl.pallas_call(
        last_body,
        out_shape=shapes(outs),
        in_specs=[vmem] * 11,
        out_specs=[hbm, vmem, vmem],
        scratch_shapes=buffers([FIELD, FIELD, SIDE, SIDE, ((3, 256, 512), F32)])
        + [pltpu.SemaphoreType.DMA((6,))],
        compiler_params=pltpu.CompilerParams(vmem_limit_bytes=32 * 1024 * 1024),
    )(*passed, shares, freq.reshape(6, 1), barrier.reshape(6, 1))
    return out.reshape(flow.shape), cnew, snew


def solution(mesh):
    placed = (
        P(None, "ax", "xs", None, None),
        P("ax", "xs", None, None),
        P(None, "ax", "xs", None, None),
        P("ax", "xs", None, None),
        P(None, ("ax", "xs")),
        P(None, ("ax", "xs")),
        P(("ax", "xs"), None),
        P(("ax", "xs")),
        P(None, ("ax", "xs")),
        P(),
        P(),
    )
    return jax.shard_map(
        local,
        mesh=mesh,
        in_specs=placed,
        out_specs=(P(None, "ax", "xs", None, None), P(None, ("ax", "xs")), P(None, ("ax", "xs"))),
        check_vma=False,
    )
```

time: 144 us -> 74 us (0.51)
  starting transfers between devices: 73.9 us -> 0 us
  Pallas kernels: 47.2 us -> 64.1 us
  waiting for transfers between devices: 7.94 us -> 0 us
  local copies, waits for them, and re-layouts: 13.3 us -> 8.74 us
    ppermute x16 -> x0, starting transfers between devices: 53.5 us -> none  [the longest x8 31.7 us: shift(): return lax.ppermute(value, ('ax', 'xs'), pairs)]
    all_to_all x2 -> x0, starting transfers between devices: 20.3 us -> none  [the longest x1 10.2 us: local(): lax.all_to_all(payload, ('ax', 'xs'), split_axis=0, concat_axis=0, tiled=...]
    pallas_call x6 -> x2, Pallas kernels: 47.2 us -> 64.1 us  [the longest x1 59.3 us: local(): pl.pallas_call(functools.partial(main_body, n_ax, n_xs), out_shape=shapes...]
    ppermute x16 -> x0, waiting for transfers between devices: 7.94 us -> none  [the longest x4 7.91 us: shift(): return lax.ppermute(value, 'ax', pairs)]
    unnamed x40 -> x18, local copies, waits for them, and re-layouts: 11.1 us -> 7.26 us
    all_to_all x2 -> x0, local copies, waits for them, and re-layouts: 1.96 us -> none  [the longest x1 0.99 us: local(): lax.all_to_all(values, ('ax', 'xs'), split_axis=0, concat_axis=0, tiled=T...]
  transfers between devices with their start and end apart: 18 -> 0, of which waited for: 2 -> 0; matrix products, arithmetic and copies ran while one was open for 2% -> 0% of each run, Pallas kernels for 25% -> 0%
where the time goes in v1:
time: 74 us; the launch traced here: 73.5 us
  Pallas kernels  64.1 us (87%)
  local copies, waits for them, and re-layouts  8.74 us (12%)
    pallas_call x1, Pallas kernels, local(): pl.pallas_call(functools.partial(main_body, n_ax, n_xs), out_shape=shapes...  59.3 us
    unnamed x18, local copies, waits for them, and re-layouts  7.26 us
    pallas_call x1, Pallas kernels, local(): pl.pallas_call(last_body, out_shape=shapes(outs), in_specs=[vmem] * 11, o...  4.75 us

profile of v1, /device:TPU:1, one launch (start us, length us, event | category | flops | bytes accessed | tf_op | source)
XLA Modules:
  0.0 73.5 jit_solution(10572042500415075151)
XLA Ops:
  0.6 0.7 %copy.14.freq = f32[6,1]{1,0:T(8,128)S(1)} copy(f32[6,1]{0,1:T(1,128)} %bitcast.15) | data formatting | bytes 48 | tf_op jit(solution)/shard_map/reshape | solution.py:572
  1.4 0.7 %copy.15.barrier = f32[6,1]{1,0:T(8,128)S(1)} copy(f32[6,1]{0,1:T(1,128)} %bitcast.16) | data formatting | bytes 48 | tf_op jit(solution)/shard_map/reshape | solution.py:572
  2.1 0.0 copy-start.1
  2.1 59.3 %shard_map.130 = (f32[3,512,256]{2,1,0:T(8,128)}, f32[3,64,128]{2,1,0:T(8,128)}, f32[3,64,128]{2,1,0:T(8,128)}, f32[3,2,2,8,128]{4,3,2,1,0:T(8,128)}, f32[3,2,2,...) custom-call(bf16[3,256,512]{2,1,0:T(8,128)(2,1)} %bitcast.10, ...), custom_call_target="tpu_custom_call" | custom-call | tf_op jit(solution)/shard_map/pallas_call | solution.py:541
  61.5 0.0 copy-done.1
  61.5 0.0 copy-start
  61.5 1.4 %copy-done = f32[3,512,256]{2,1,0:T(8,128)S(1)} copy-done((f32[3,512,256]{2,1,0:T(8,128)S(1)}, f32[3,512,256]{2,1,0:T(8,128)}, u32[]{:S(2)}) %copy-start) | copy-done | bytes 1572888
  62.9 0.0 copy-start.2
  62.9 0.9 %copy-done.2 = f32[3,64,128]{2,1,0:T(8,128)S(1)} copy-done((f32[3,64,128]{2,1,0:T(8,128)S(1)}, f32[3,64,128]{2,1,0:T(8,128)}, u32[]{:S(2)}) %copy-start.2) | copy-done | bytes 98328
  63.8 0.0 copy-start.3
  63.8 0.9 %copy-done.3 = f32[3,64,128]{2,1,0:T(8,128)S(1)} copy-done((f32[3,64,128]{2,1,0:T(8,128)S(1)}, f32[3,64,128]{2,1,0:T(8,128)}, u32[]{:S(2)}) %copy-start.3) | copy-done | bytes 98328
  64.7 0.0 copy-start.4
  64.7 0.8 %copy-done.4 = f32[4,4096]{1,0:T(4,128)S(1)} copy-done((f32[4,4096]{1,0:T(4,128)S(1)}, f32[4,4096]{1,0:T(4,128)}, u32[]{:S(2)}) %copy-start.4) | copy-done | bytes 65560
  65.5 0.0 copy-start.5
  65.5 0.8 %copy-done.5 = f32[3,4096]{1,0:T(4,128)S(1)} copy-done((f32[3,4096]{1,0:T(4,128)S(1)}, f32[3,4096]{1,0:T(4,128)}, u32[]{:S(2)}) %copy-start.5) | copy-done | bytes 49176
  66.4 0.0 copy-start.6
  66.4 0.8 %copy-done.6 = f32[3,2,2,8,128]{4,3,2,1,0:T(8,128)S(1)} copy-done((f32[3,2,2,8,128]{4,3,2,1,0:T(8,128)S(1)}, f32[3,2,2,8,128]{4,3,2,1,0:T(8,128)}, u32[]{:S(2)}) %copy-start.6) | copy-done | bytes 49176
  67.2 0.0 copy-start.7
  67.2 0.8 %copy-done.7 = f32[3,2,2,8,128]{4,3,2,1,0:T(8,128)S(1)} copy-done((f32[3,2,2,8,128]{4,3,2,1,0:T(8,128)S(1)}, f32[3,2,2,8,128]{4,3,2,1,0:T(8,128)}, u32[]{:S(2)}) %copy-start.7) | copy-done | bytes 49176
  68.0 0.0 copy-start.8
  68.0 0.8 %copy-done.8 = f32[4,3,8,128]{3,2,1,0:T(8,128)S(1)} copy-done((f32[4,3,8,128]{3,2,1,0:T(8,128)S(1)}, f32[4,3,8,128]{3,2,1,0:T(8,128)}, u32[]{:S(2)}) %copy-start.8) | copy-done | bytes 49176
  68.8 4.7 %shard_map.131 = (f32[3,256,512]{2,1,0:T(8,128)}, f32[3,4096]{1,0:T(4,128)}, f32[6,4096]{1,0:T(8,128)}) custom-call(f32[3,512,256]{2,1,0:T(8,128)S(1)} %copy-done, f32[3,64,128]{2,1,0:T(8,128)S(1)} %copy-done.2, f32[3,64,128]{2,1,0:T(8,128)S(1)} %copy-done.3, f32[3,2,2,8,128]{4,3,2,1,0:T(8,128)S(1)} %copy-done.6, f32[3,2,2,8,128]{4,3,2,1,0:T(8,128)S(1)} %copy-done.7, ...), custom_call_target="tpu_custom_call" | custom-call | tf_op jit(solution)/shard_map/pallas_call | solution.py:564
Async XLA Ops:
  2.1 59.4 %copy-start.1 = (f32[6,4096]{1,0:T(8,128)S(1)}, f32[6,4096]{1,0:T(8,128)}, u32[]{:S(2)}) copy-start(f32[6,4096]{1,0:T(8,128)} %shares.1) | copy-start | bytes 294916
  61.5 1.4 %copy-start = (f32[3,512,256]{2,1,0:T(8,128)S(1)}, f32[3,512,256]{2,1,0:T(8,128)}, u32[]{:S(2)}) copy-start(f32[3,512,256]{2,1,0:T(8,128)} %get-tuple-element.14.h1) | copy-start | bytes 4718596
  62.9 0.9 %copy-start.2 = (f32[3,64,128]{2,1,0:T(8,128)S(1)}, f32[3,64,128]{2,1,0:T(8,128)}, u32[]{:S(2)}) copy-start(f32[3,64,128]{2,1,0:T(8,128)} %get-tuple-element.15.low1) | copy-start | bytes 294916
  63.8 0.9 %copy-start.3 = (f32[3,64,128]{2,1,0:T(8,128)S(1)}, f32[3,64,128]{2,1,0:T(8,128)}, u32[]{:S(2)}) copy-start(f32[3,64,128]{2,1,0:T(8,128)} %get-tuple-element.16.high1) | copy-start | bytes 294916
  64.7 0.8 %copy-start.4 = (f32[4,4096]{1,0:T(4,128)S(1)}, f32[4,4096]{1,0:T(4,128)}, u32[]{:S(2)}) copy-start(f32[4,4096]{1,0:T(4,128)} %get-tuple-element.20.probe) | copy-start | bytes 196612
  65.5 0.8 %copy-start.5 = (f32[3,4096]{1,0:T(4,128)S(1)}, f32[3,4096]{1,0:T(4,128)}, u32[]{:S(2)}) copy-start(f32[3,4096]{1,0:T(4,128)} %get-tuple-element.21.coords) | copy-start | bytes 147460
  66.4 0.8 %copy-start.6 = (f32[3,2,2,8,128]{4,3,2,1,0:T(8,128)S(1)}, f32[3,2,2,8,128]{4,3,2,1,0:T(8,128)}, u32[]{:S(2)}) copy-start(f32[3,2,2,8,128]{4,3,2,1,0:T(8,128)} %get-tuple-element.17.left1) | copy-start | bytes 147460
  67.2 0.8 %copy-start.7 = (f32[3,2,2,8,128]{4,3,2,1,0:T(8,128)S(1)}, f32[3,2,2,8,128]{4,3,2,1,0:T(8,128)}, u32[]{:S(2)}) copy-start(f32[3,2,2,8,128]{4,3,2,1,0:T(8,128)} %get-tuple-element.18.right1) | copy-start | bytes 147460
  68.0 0.8 %copy-start.8 = (f32[4,3,8,128]{3,2,1,0:T(8,128)S(1)}, f32[4,3,8,128]{3,2,1,0:T(8,128)}, u32[]{:S(2)}) copy-start(f32[4,3,8,128]{3,2,1,0:T(8,128)} %get-tuple-element.19.corners) | copy-start | bytes 147460

commit v2 on v1

--- a/solution.py
+++ b/solution.py
@@ -159,11 +159,12 @@
         third = jnp.concatenate(
             [lag_ref[pl.ds(128 + s0, 8, stride=8), :], lag_ref[pl.ds(128 + s1, 8, stride=8), :]], 1
         )
+        rows = jnp.dot(table_ref[...], hot, preferred_element_type=F32)
         for f in range(4):
-            rows = jnp.dot(table_ref[pl.ds(f * 512, 512), :], hot, preferred_element_type=F32)
             one = None
             for i in range(8):
-                term = rows[i * 64 : (i + 1) * 64] * weight(0, i)
+                at = f * 512 + i * 64
+                term = rows[at : at + 64] * weight(0, i)
                 one = term if one is None else one + term
             two = None
             for j in range(8):
@@ -195,8 +196,14 @@
 
 def kinetics(probe_ref, coords_ref, share_ref, freq_ref, barrier_ref, cnew_ref, snew_ref):
     cnew_ref[...] = coords_ref[...] + STEP_DT * probe_ref[0:3, :]
-    rates = freq_ref[...] * jnp.exp(barrier_ref[...] * jnp.tanh(probe_ref[3:4, :] - 1.0))
     shares = share_ref[...]
+    species = lax.broadcasted_iota(jnp.int32, shares.shape, 0)
+    freq = jnp.full(shares.shape, freq_ref[0], F32)
+    barrier = jnp.full(shares.shape, barrier_ref[0], F32)
+    for q in range(1, 6):
+        freq = jnp.where(species == q, freq_ref[q], freq)
+        barrier = jnp.where(species == q, barrier_ref[q], barrier)
+    rates = freq * jnp.exp(barrier * jnp.tanh(probe_ref[3:4, :] - 1.0))
     flux = rates * shares
     moved = jnp.concatenate([flux[5:6], flux[0:5]], 0)
     snew_ref[...] = shares + STEP_DT * (moved - flux)
@@ -277,13 +284,30 @@
     lax.fori_loop(0, 6, pack, 0)
 
 
-def assemble(h_ref, x_ref, low_ref, high_ref, left_ref, right_ref, corner_ref, lowest, highest):
-    lane = lax.broadcasted_iota(jnp.int32, (8, 128), 1)
+def radially(x):
+    lane = lax.broadcasted_iota(jnp.int32, (8, 128), 1) % 32
     sub = lax.broadcasted_iota(jnp.int32, (8, 128), 0)
-    quarter, radial = lane // 32, lane % 32
-    at_first = (sub == 0) & (radial != 0)
-    at_last = (sub == 7) & (radial != 31)
-
+    up = pltpu.roll(pltpu.roll(x, 1, 1), 1, 0)
+    down = pltpu.roll(pltpu.roll(x, 127, 1), 7, 0)
+    x = x + jnp.where((sub == 0) & (lane != 0), up, 0.0)
+    return x + jnp.where((sub == 7) & (lane != 31), down, 0.0)
+
+
+def assemble_inside(h_ref, x_ref):
+    def part(n, carry):
+        f, a = n // 2, n % 2
+        lanes = pl.ds(pl.multiple_of(a * 128, 128), 128)
+        for i in range(1, 7):
+            for j in range(1, 7):
+                row = pl.ds(i * 64 + j * 8, 8)
+                x_ref[f, row, lanes] = radially(h_ref[f, row, lanes])
+        return carry
+
+    lax.fori_loop(0, 6, part, 0)
+
+
+def assemble_rim(h_ref, x_ref, low_ref, high_ref, left_ref, right_ref, corner_ref, lowest, highest):
+    quarter = lax.broadcasted_iota(jnp.int32, (8, 128), 1) // 32
     under = jnp.where(lowest, F32(0.0), F32(1.0))
     over = jnp.where(highest, F32(0.0), F32(1.0))
 
@@ -300,11 +324,6 @@
         return carry
 
     lax.fori_loop(0, 3, near, 0)
-
-    def radially(x):
-        up = pltpu.roll(pltpu.roll(x, 1, 1), 1, 0)
-        down = pltpu.roll(pltpu.roll(x, 127, 1), 7, 0)
-        return x + jnp.where(at_first, up, 0.0) + jnp.where(at_last, down, 0.0)
 
     def part(n, carry):
         f, a = n // 2, n % 2
@@ -322,6 +341,7 @@
             after = jnp.where(quarter == 3, after, pltpu.roll(first, 96, 1))
             x_ref[f, pl.ds(i * 64, 8), lanes] = radially(first + before)
             x_ref[f, pl.ds(i * 64 + 56, 8), lanes] = radially(last + after)
+        for i in (0, 7):
             for j in range(1, 7):
                 row = pl.ds(i * 64 + j * 8, 8)
                 x_ref[f, row, lanes] = radially(h_ref[f, row, lanes])
@@ -337,7 +357,7 @@
 RIMS = [FACE, FACE, SIDE, SIDE]
 SLOTS = ((128, 4, 128), F32)
 MESH = pl.DeviceIdType.MESH
-LIMIT = 56 * 1024 * 1024
+LIMIT = 40 * 1024 * 1024
 
 
 def rim_copies(n_ax, n_xs, sent, landed, corners, send_sems, recv_sems):
@@ -368,11 +388,11 @@
 
 def main_body(n_ax, n_xs, *refs):
     (flow_h, heat_h, stiff_h, inert_h, idx_h, off_h, own_h, piece_h) = refs[:8]
-    (h2, low4, high4, left4, right4, corners2, probe, coords) = refs[8:16]
-    (flow, heat, stiff, inert, idx, off, own, piece) = refs[16:24]
-    (rank, pay, got, back, ret, x, h, g, c, table, tables, lag, halves) = refs[24:37]
-    (low1, high1, left1, right1, low2, high2, left2, right2, corners1) = refs[37:46]
-    (low3, high3, left3, right3) = refs[46:50]
+    x2, probe, coords = refs[8:11]
+    (flow, heat, stiff, inert, idx, off, own, piece) = refs[11:19]
+    (rank, pay, got, back, ret, x, h, g, c, table, tables, lag, halves) = refs[19:32]
+    (low1, high1, left1, right1, low2, high2, left2, right2, corners1) = refs[32:41]
+    (low3, high3, left3, right3, low4, high4, left4, right4, corners2) = refs[41:50]
     (in_sems, out_send, out_recv, back_send, back_recv, rim_send, rim_recv) = refs[50:]
     devices = n_ax * n_xs
     ax, xs = lax.axis_index("ax"), lax.axis_index("xs")
@@ -470,11 +490,12 @@
 
     lax.fori_loop(0, devices // 8, block, 0)
 
+    assemble_inside(h, x)
     for copy in first:
         copy.wait()
-    assemble(h, x, low2, high2, left2, right2, corners1, ax == 0, ax == n_ax - 1)
-    helm(x, g, c, tables, h2)
-    faces(h2, low3, high3, left3, right3)
+    assemble_rim(h, x, low2, high2, left2, right2, corners1, ax == 0, ax == n_ax - 1)
+    helm(x, g, c, tables, h)
+    faces(h, low3, high3, left3, right3)
     second = rim_copies(
         n_ax, n_xs, (low3, high3, left3, right3), (low4, high4, left4, right4), corners2,
         rim_send.at[1], rim_recv.at[1],
@@ -484,21 +505,17 @@
 
     pltpu.make_async_copy(ret, ret, back_recv).wait()
     gather_back(ret, own, rank, probe, halves)
+    assemble_inside(h, x2)
 
     others = pl.ds(0, devices - 1)
     pltpu.make_async_copy(pay.at[others], pay.at[others], out_send).wait()
     pltpu.make_async_copy(back.at[others], back.at[others], back_send).wait()
     for copy in second:
         copy.wait()
-
-
-def last_body(h1, low1, high1, left1, right1, corners, probe, coords, shares, freq, barrier, out, cnew, snew, x, work, l1, r1, turned, sems):
-    ax, n_ax = lax.axis_index("ax"), lax.axis_size("ax")
-    kinetics(probe, coords, shares, freq, barrier, cnew, snew)
-    work[...] = h1[...]
-    l1[...] = left1[...]
-    r1[...] = right1[...]
-    assemble(work, x, low1, high1, l1, r1, corners, ax == 0, ax == n_ax - 1)
+    assemble_rim(h, x2, low4, high4, left4, right4, corners2, ax == 0, ax == n_ax - 1)
+
+
+def last_body(x, probe, coords, shares, freq, barrier, out, cnew, snew, turned, sems):
     copies = []
     for d in range(3):
         for a in range(2):
@@ -507,6 +524,7 @@
             copy = pltpu.make_async_copy(turned.at[d, lanes], out.at[d, lanes], sems.at[d * 2 + a])
             copy.start()
             copies.append(copy)
+    kinetics(probe, coords, shares, freq, barrier, cnew, snew)
     for copy in copies:
         copy.wait()
 
@@ -525,6 +543,7 @@
     devices = n_ax * n_xs
     vmem = pl.BlockSpec(memory_space=pltpu.VMEM)
     hbm = pl.BlockSpec(memory_space=pltpu.HBM)
+    smem = pl.BlockSpec(memory_space=pltpu.SMEM)
     inputs = (
         flow.reshape(3, 256, 512),
         heat.reshape(256, 512),
@@ -535,9 +554,10 @@
         owner.reshape(1, particles),
         piece.reshape(1, particles),
     )
+    inputs = [pltpu.with_memory_space_constraint(a, pltpu.HBM) for a in inputs]
     held = [(a.shape, a.dtype) for a in inputs]
     table = ((2048, 256), BF16)
-    outs = [FIELD, *RIMS, CORNER, ((4, particles), F32), ((3, particles), F32)]
+    outs = [FIELD, ((4, particles), F32), ((3, particles), F32)]
     passed = pl.pallas_call(
         functools.partial(main_body, n_ax, n_xs),
         out_shape=shapes(outs),
@@ -546,7 +566,7 @@
         scratch_shapes=buffers(held)
         + buffers([((1, particles), jnp.int32), SLOTS, SLOTS, SLOTS, SLOTS, FIELD, FIELD, FIELD])
         + buffers([((512, 256), F32), table, ((16, 8, 128), F32), ((192, 128), F32), ((512, 256), BF16)])
-        + buffers([*RIMS, *RIMS, CORNER, *RIMS])
+        + buffers([*RIMS, *RIMS, CORNER, *RIMS, *RIMS, CORNER])
         + [
             pltpu.SemaphoreType.DMA((8,)),
             pltpu.SemaphoreType.DMA,
@@ -564,12 +584,12 @@
     out, cnew, snew = pl.pallas_call(
         last_body,
         out_shape=shapes(outs),
-        in_specs=[vmem] * 11,
+        in_specs=[vmem] * 4 + [smem] * 2,
         out_specs=[hbm, vmem, vmem],
-        scratch_shapes=buffers([FIELD, FIELD, SIDE, SIDE, ((3, 256, 512), F32)])
+        scratch_shapes=buffers([((3, 256, 512), F32)])
         + [pltpu.SemaphoreType.DMA((6,))],
-        compiler_params=pltpu.CompilerParams(vmem_limit_bytes=32 * 1024 * 1024),
-    )(*passed, shares, freq.reshape(6, 1), barrier.reshape(6, 1))
+        compiler_params=pltpu.CompilerParams(vmem_limit_bytes=8 * 1024 * 1024),
+    )(*passed, shares, freq, barrier)
     return out.reshape(flow.shape), cnew, snew
 
 

time: 74 us -> 60.9 us (0.82)
  local copies, waits for them, and re-layouts: 8.74 us -> 0.01 us
  Pallas kernels: 64.1 us -> 60.1 us
    unnamed x18 -> x6, local copies, waits for them, and re-layouts: 7.26 us -> 0.01 us
    pallas_call x1, Pallas kernels: 4.75 us -> 2.54 us  [local(): pl.pallas_call(last_body, out_shape=shapes(outs), in_specs=[vmem] * 4 + [...]
    pallas_call x1, Pallas kernels: 59.3 us -> 57.6 us  [local(): pl.pallas_call(functools.partial(main_body, n_ax, n_xs), out_shape=shapes...]
    reshape x2 -> x0, local copies, waits for them, and re-layouts: 1.48 us -> none  [the longest x1 0.74 us: local(): freq.reshape(6, 1)]
where the time goes in v2:
time: 60.9 us; the launch traced here: 60.8 us
  Pallas kernels  60.1 us (99%)
  between operations  0.69 us (1%)
    pallas_call x1, Pallas kernels, local(): pl.pallas_call(functools.partial(main_body, n_ax, n_xs), out_shape=shapes...  57.6 us
    pallas_call x1, Pallas kernels, local(): pl.pallas_call(last_body, out_shape=shapes(outs), in_specs=[vmem] * 4 + [...  2.54 us

profile of v2, /device:TPU:1, one launch (start us, length us, event | category | flops | bytes accessed | tf_op | source)
XLA Modules:
  0.0 60.8 jit_solution(6987740179550464043)
XLA Ops:
  0.6 0.0 copy-start
  0.6 0.0 copy-start.1
  0.7 0.0 copy-start.2
  0.7 57.6 %shard_map.130 = (f32[3,512,256]{2,1,0:T(8,128)S(1)}, f32[4,4096]{1,0:T(4,128)S(1)}, f32[3,4096]{1,0:T(4,128)S(1)}) custom-call(bf16[3,256,512]{2,1,0:T(8,128)(2,1)} %bitcast.8, bf16[256,512]{1,0:T(8,128)(2,1)} %bitcast.10, f32[3,256,512]{2,1,0:T(8,128)} %bitcast.7, f32[256,512]{1,0:T(8,128)} %bitcast.9, s32[3,4096]{1,0:T(4,128)} %refs_4_.1, ...), custom_call_target="tpu_custom_call" | custom-call | tf_op jit(solution)/shard_map/pallas_call | solution.py:561
  58.2 0.0 copy-done
  58.3 0.0 copy-done.1
  58.3 0.0 copy-done.2
  58.3 2.5 %shard_map.131 = (f32[3,256,512]{2,1,0:T(8,128)}, f32[3,4096]{1,0:T(4,128)}, f32[6,4096]{1,0:T(8,128)}) custom-call(f32[3,512,256]{2,1,0:T(8,128)S(1)} %get-tuple-element.9.x, f32[4,4096]{1,0:T(4,128)S(1)} %get-tuple-element.10.probe, f32[3,4096]{1,0:T(4,128)S(1)} %get-tuple-element.11.coords, f32[6,4096]{1,0:T(8,128)S(1)} %copy-done, f32[6]{0:T(128)S(1)} %copy-done.1, ...), custom_call_target="tpu_custom_call" | custom-call | tf_op jit(solution)/shard_map/pallas_call | solution.py:584
Async XLA Ops:
  0.6 57.6 %copy-start = (f32[6,4096]{1,0:T(8,128)S(1)}, f32[6,4096]{1,0:T(8,128)}, u32[]{:S(2)}) copy-start(f32[6,4096]{1,0:T(8,128)} %shares.1) | copy-start | bytes 294916
  0.6 57.6 %copy-start.1 = (f32[6]{0:T(128)S(1)}, f32[6]{0:T(128)}, u32[]{:S(2)}) copy-start(f32[6]{0:T(128)} %freq.1) | copy-start | bytes 76
  0.7 57.6 %copy-start.2 = (f32[6]{0:T(128)S(1)}, f32[6]{0:T(128)}, u32[]{:S(2)}) copy-start(f32[6]{0:T(128)} %barrier.1) | copy-start | bytes 76

commit v3 on v2

--- a/solution.py
+++ b/solution.py
@@ -350,6 +350,16 @@
     lax.fori_loop(0, 6, part, 0)
 
 
+def turn_out(x_ref, out_ref):
+    def three(d, carry):
+        for a in range(2):
+            lanes = pl.ds(a * 128, 128)
+            out_ref[d, lanes, :] = jnp.transpose(x_ref[d, :, lanes])
+        return carry
+
+    lax.fori_loop(0, 3, three, 0)
+
+
 FIELD = ((3, 512, 256), F32)
 FACE = ((3, 64, 128), F32)
 SIDE = ((3, 2, 2, 8, 128), F32)
@@ -388,7 +398,7 @@
 
 def main_body(n_ax, n_xs, *refs):
     (flow_h, heat_h, stiff_h, inert_h, idx_h, off_h, own_h, piece_h) = refs[:8]
-    x2, probe, coords = refs[8:11]
+    turned, probe, coords = refs[8:11]
     (flow, heat, stiff, inert, idx, off, own, piece) = refs[11:19]
     (rank, pay, got, back, ret, x, h, g, c, table, tables, lag, halves) = refs[19:32]
     (low1, high1, left1, right1, low2, high2, left2, right2, corners1) = refs[32:41]
@@ -428,8 +438,7 @@
     dispatch(idx, off, own, piece, coords, rank, pay)
     pl.semaphore_wait(barrier, devices - 1)
 
-    group = lax.div(me, 8)
-    own_copy = pltpu.make_async_copy(pay.at[me], got.at[me], out_recv.at[group])
+    own_copy = pltpu.make_async_copy(pay.at[me], got.at[me], out_recv.at[ax])
     own_copy.start()
 
     def send(k, carry):
@@ -438,7 +447,7 @@
             src_ref=pay.at[to],
             dst_ref=got.at[me],
             send_sem=out_send,
-            recv_sem=out_recv.at[group],
+            recv_sem=out_recv.at[ax],
             device_id=where(to),
             device_id_type=MESH,
         ).start()
@@ -459,11 +468,12 @@
         copy.start()
 
     def block(n, carry):
-        now = lax.rem(group + 2 * (devices // 8) - 1 - n, devices // 8)
-        base = now * 8
-        rows = got.at[pl.ds(base, 8)]
+        now = lax.rem(ax + 2 * n_ax - 1 - n, n_ax)
+        base = now * n_xs
+        rows = got.at[pl.ds(base, n_xs)]
         pltpu.make_async_copy(rows, rows, out_recv.at[now]).wait()
-        interpolate(base, got, table, back, lag)
+        for part in range(n_xs // 8):
+            interpolate(base + part * 8, got, table, back, lag.at[part])
 
         def give(s, inner):
             to = base + s
@@ -475,7 +485,7 @@
                     dst_ref=ret.at[me],
                     send_sem=back_send,
                     recv_sem=back_recv,
-                    device_id=where(to),
+                    device_id=(now, s),
                     device_id_type=MESH,
                 ).start()
 
@@ -485,11 +495,10 @@
 
             return inner
 
-        lax.fori_loop(0, 8, give, 0)
-        return carry
-
-    lax.fori_loop(0, devices // 8, block, 0)
-
+        lax.fori_loop(0, n_xs, give, 0)
+        return carry
+
+    lax.fori_loop(0, n_ax // 4, block, 0)
     assemble_inside(h, x)
     for copy in first:
         copy.wait()
@@ -502,31 +511,26 @@
     )
     for copy in second:
         copy.start()
-
+    lax.fori_loop(n_ax // 4, n_ax, block, 0)
+
+    assemble_inside(h, x)
+    for copy in second:
+        copy.wait()
+    assemble_rim(h, x, low4, high4, left4, right4, corners2, ax == 0, ax == n_ax - 1)
+    turn_out(x, turned)
     pltpu.make_async_copy(ret, ret, back_recv).wait()
     gather_back(ret, own, rank, probe, halves)
-    assemble_inside(h, x2)
 
     others = pl.ds(0, devices - 1)
     pltpu.make_async_copy(pay.at[others], pay.at[others], out_send).wait()
     pltpu.make_async_copy(back.at[others], back.at[others], back_send).wait()
-    for copy in second:
-        copy.wait()
-    assemble_rim(h, x2, low4, high4, left4, right4, corners2, ax == 0, ax == n_ax - 1)
-
-
-def last_body(x, probe, coords, shares, freq, barrier, out, cnew, snew, turned, sems):
-    copies = []
-    for d in range(3):
-        for a in range(2):
-            lanes = pl.ds(a * 128, 128)
-            turned[d, lanes, :] = jnp.transpose(x[d, :, lanes])
-            copy = pltpu.make_async_copy(turned.at[d, lanes], out.at[d, lanes], sems.at[d * 2 + a])
-            copy.start()
-            copies.append(copy)
+
+
+def last_body(turned, probe, coords, shares, freq, barrier, out, cnew, snew, sem):
+    copy = pltpu.make_async_copy(turned, out, sem)
+    copy.start()
     kinetics(probe, coords, shares, freq, barrier, cnew, snew)
-    for copy in copies:
-        copy.wait()
+    copy.wait()
 
 
 def shapes(outs):
@@ -557,7 +561,7 @@
     inputs = [pltpu.with_memory_space_constraint(a, pltpu.HBM) for a in inputs]
     held = [(a.shape, a.dtype) for a in inputs]
     table = ((2048, 256), BF16)
-    outs = [FIELD, ((4, particles), F32), ((3, particles), F32)]
+    outs = [((3, 256, 512), F32), ((4, particles), F32), ((3, particles), F32)]
     passed = pl.pallas_call(
         functools.partial(main_body, n_ax, n_xs),
         out_shape=shapes(outs),
@@ -565,12 +569,12 @@
         out_specs=[vmem] * len(outs),
         scratch_shapes=buffers(held)
         + buffers([((1, particles), jnp.int32), SLOTS, SLOTS, SLOTS, SLOTS, FIELD, FIELD, FIELD])
-        + buffers([((512, 256), F32), table, ((16, 8, 128), F32), ((192, 128), F32), ((512, 256), BF16)])
+        + buffers([((512, 256), F32), table, ((16, 8, 128), F32), ((2, 192, 128), F32), ((512, 256), BF16)])
         + buffers([*RIMS, *RIMS, CORNER, *RIMS, *RIMS, CORNER])
         + [
             pltpu.SemaphoreType.DMA((8,)),
             pltpu.SemaphoreType.DMA,
-            pltpu.SemaphoreType.DMA((devices // 8,)),
+            pltpu.SemaphoreType.DMA((n_ax,)),
             pltpu.SemaphoreType.DMA,
             pltpu.SemaphoreType.DMA,
             pltpu.SemaphoreType.DMA((2, 8)),
@@ -586,8 +590,7 @@
         out_shape=shapes(outs),
         in_specs=[vmem] * 4 + [smem] * 2,
         out_specs=[hbm, vmem, vmem],
-        scratch_shapes=buffers([((3, 256, 512), F32)])
-        + [pltpu.SemaphoreType.DMA((6,))],
+        scratch_shapes=[pltpu.SemaphoreType.DMA],
         compiler_params=pltpu.CompilerParams(vmem_limit_bytes=8 * 1024 * 1024),
     )(*passed, shares, freq, barrier)
     return out.reshape(flow.shape), cnew, snew

time: 60.9 us -> 57.9 us (0.951)
  Pallas kernels: 60.1 us -> 57.1 us
    pallas_call x1, Pallas kernels: 57.6 us -> 54.8 us  [local(): pl.pallas_call(functools.partial(main_body, n_ax, n_xs), out_shape=shapes...]
where the time goes in v3:
time: 57.9 us; the launch traced here: 57.8 us
  Pallas kernels  57.1 us (99%)
  between operations  0.69 us (1%)
    pallas_call x1, Pallas kernels, local(): pl.pallas_call(functools.partial(main_body, n_ax, n_xs), out_shape=shapes...  54.8 us
    pallas_call x1, Pallas kernels, local(): pl.pallas_call(last_body, out_shape=shapes(outs), in_specs=[vmem] * 4 + [...  2.37 us

profile of v3, /device:TPU:1, one launch (start us, length us, event | category | flops | bytes accessed | tf_op | source)
XLA Modules:
  0.0 57.8 jit_solution(1937247461980221997)
XLA Ops:
  0.6 0.0 copy-start
  0.6 0.0 copy-start.1
  0.7 0.0 copy-start.2
  0.7 54.8 %shard_map.130 = (f32[3,256,512]{2,1,0:T(8,128)S(1)}, f32[4,4096]{1,0:T(4,128)S(1)}, f32[3,4096]{1,0:T(4,128)S(1)}) custom-call(bf16[3,256,512]{2,1,0:T(8,128)(2,1)} %bitcast.8, bf16[256,512]{1,0:T(8,128)(2,1)} %bitcast.10, f32[3,256,512]{2,1,0:T(8,128)} %bitcast.7, f32[256,512]{1,0:T(8,128)} %bitcast.9, s32[3,4096]{1,0:T(4,128)} %refs_4_.1, ...), custom_call_target="tpu_custom_call" | custom-call | tf_op jit(solution)/shard_map/pallas_call | solution.py:565
  55.4 0.0 copy-done
  55.4 0.0 copy-done.1
  55.4 0.0 copy-done.2
  55.5 2.4 %shard_map.131 = (f32[3,256,512]{2,1,0:T(8,128)}, f32[3,4096]{1,0:T(4,128)}, f32[6,4096]{1,0:T(8,128)}) custom-call(f32[3,256,512]{2,1,0:T(8,128)S(1)} %get-tuple-element.9.turned, f32[4,4096]{1,0:T(4,128)S(1)} %get-tuple-element.10.probe, f32[3,4096]{1,0:T(4,128)S(1)} %get-tuple-element.11.coords, f32[6,4096]{1,0:T(8,128)S(1)} %copy-done, f32[6]{0:T(128)S(1)} %copy-done.1, ...), custom_call_target="tpu_custom_call" | custom-call | tf_op jit(solution)/shard_map/pallas_call | solution.py:588
Async XLA Ops:
  0.6 54.8 %copy-start = (f32[6,4096]{1,0:T(8,128)S(1)}, f32[6,4096]{1,0:T(8,128)}, u32[]{:S(2)}) copy-start(f32[6,4096]{1,0:T(8,128)} %shares.1) | copy-start | bytes 294916
  0.6 54.8 %copy-start.1 = (f32[6]{0:T(128)S(1)}, f32[6]{0:T(128)}, u32[]{:S(2)}) copy-start(f32[6]{0:T(128)} %freq.1) | copy-start | bytes 76
  0.7 54.8 %copy-start.2 = (f32[6]{0:T(128)S(1)}, f32[6]{0:T(128)}, u32[]{:S(2)}) copy-start(f32[6]{0:T(128)} %barrier.1) | copy-start | bytes 76

commit v4 on v3

--- a/solution.py
+++ b/solution.py
@@ -46,16 +46,6 @@
 DM = np.asarray(deriv_table(), np.float32).astype(np.float64)
 
 
-def fill_tables(t_ref):
-    sub = lax.broadcasted_iota(jnp.int32, (8, 128), 0)
-    for half, table in enumerate((DM, DM.T)):
-        for s in range(8):
-            out = jnp.full((8, 128), table[0, (0 - s) % 8], F32)
-            for p in range(1, 8):
-                out = jnp.where(sub == p, F32(table[p, (p - s) % 8]), out)
-            t_ref[half * 8 + s] = out
-
-
 def apply_table(table, u):
     even = [u[i] + u[7 - i] for i in range(4)]
     odd = [u[i] - u[7 - i] for i in range(4)]
@@ -70,13 +60,6 @@
             b = tb if b is None else b + tb
         out[p], out[7 - p] = a + b, b - a
     return out
-
-
-def apply_rolls(tables, x):
-    y = x * tables[0]
-    for s in range(1, 8):
-        y = y + pltpu.roll(x, s, 0) * tables[s]
-    return y
 
 
 def pick_node(cell, shift):
@@ -214,40 +197,41 @@
         for a in range(2):
             lanes = pl.ds(a * 128, 128)
             turned = jnp.transpose(flow_ref[d, lanes, :].astype(F32))
-            x_ref[d, :, lanes] = turned
+            x_ref[d * 2 + a] = turned
             table_ref[pl.ds(pl.multiple_of(d * 512, 512), 512), lanes] = turned.astype(BF16)
-            g_ref[d, :, lanes] = jnp.transpose(stiff_ref[d, lanes, :])
+            g_ref[d * 2 + a] = jnp.transpose(stiff_ref[d, lanes, :])
         return carry
 
     lax.fori_loop(0, 3, three, 0)
     for a in range(2):
         lanes = pl.ds(a * 128, 128)
         table_ref[pl.ds(1536, 512), lanes] = jnp.transpose(heat_ref[lanes, :].astype(F32)).astype(BF16)
-        c_ref[:, lanes] = jnp.transpose(inert_ref[lanes, :])
-
-
-def helm(x_ref, g_ref, c_ref, t_ref, h_ref):
+        c_ref[a] = jnp.transpose(inert_ref[lanes, :])
+
+
+def helm(x_ref, g_ref, c_ref, h_ref):
     def part(n, carry):
-        f, a = n // 2, n % 2
-        lanes = pl.ds(pl.multiple_of(a * 128, 128), 128)
-        fore = [t_ref[s] for s in range(8)]
-        aft = [t_ref[8 + s] for s in range(8)]
+        a = n % 2
+
+        def along(d, at):
+            line = apply_table(DM, [x_ref[n, p, :] for p in at])
+            return apply_table(DM.T, [g_ref[d * 2 + a, at[p], :] * line[p] for p in range(8)])
+
         for i in range(8):
             at = [pl.ds(i * 64 + j * 8, 8) for j in range(8)]
-            x = [x_ref[f, at[j], lanes] for j in range(8)]
-            dj = apply_table(DM, x)
-            dj = [g_ref[1, at[j], lanes] * dj[j] for j in range(8)]
-            dj = apply_table(DM.T, dj)
+            line = along(1, at)
             for j in range(8):
-                dk = g_ref[2, at[j], lanes] * apply_rolls(fore, x[j])
-                h_ref[f, at[j], lanes] = dj[j] + c_ref[at[j], lanes] * x[j] + apply_rolls(aft, dk)
+                h_ref[n, at[j], :] = line[j] + c_ref[a, at[j], :] * x_ref[n, at[j], :]
         for j in range(8):
             at = [pl.ds(i * 64 + j * 8, 8) for i in range(8)]
-            di = apply_table(DM, [x_ref[f, at[i], lanes] for i in range(8)])
-            di = [g_ref[0, at[i], lanes] * di[i] for i in range(8)]
-            di = apply_table(DM.T, di)
+            line = along(0, at)
             for i in range(8):
-                h_ref[f, at[i], lanes] += di[i]
+                h_ref[n, at[i], :] += line[i]
+        for i in range(8):
+            at = [pl.ds(i * 64 + k, 8, stride=8) for k in range(8)]
+            line = along(2, at)
+            for k in range(8):
+                h_ref[n, at[k], :] += line[k]
         return carry
 
     lax.fori_loop(0, 6, part, 0)
@@ -255,22 +239,21 @@
 
 def faces(h_ref, low_ref, high_ref, left_ref, right_ref):
     for f in range(3):
-        low_ref[f] = h_ref[f, 0:64, 0:128]
-        high_ref[f] = h_ref[f, 448:512, 128:256]
-        both = h_ref[f, 448:512, 0:128] + h_ref[f, 0:64, 128:256]
-        h_ref[f, 448:512, 0:128] = both
-        h_ref[f, 0:64, 128:256] = both
+        low_ref[f] = h_ref[2 * f, 0:64]
+        high_ref[f] = h_ref[2 * f + 1, 448:512]
+        both = h_ref[2 * f, 448:512] + h_ref[2 * f + 1, 0:64]
+        h_ref[2 * f, 448:512] = both
+        h_ref[2 * f + 1, 0:64] = both
     lane = lax.broadcasted_iota(jnp.int32, (8, 128), 1) // 32
 
     def pack(n, carry):
         f, a = n // 2, n % 2
-        lanes = pl.ds(pl.multiple_of(a * 128, 128), 128)
         for half in range(2):
             one = two = None
             for q in range(4):
                 row = (half * 4 + q) * 64
-                first = h_ref[f, pl.ds(row, 8), lanes]
-                last = h_ref[f, pl.ds(row + 56, 8), lanes]
+                first = h_ref[n, pl.ds(row, 8), :]
+                last = h_ref[n, pl.ds(row + 56, 8), :]
                 if q:
                     first = pltpu.roll(first, 32 * q, 1)
                 if q < 3:
@@ -284,30 +267,9 @@
     lax.fori_loop(0, 6, pack, 0)
 
 
-def radially(x):
-    lane = lax.broadcasted_iota(jnp.int32, (8, 128), 1) % 32
-    sub = lax.broadcasted_iota(jnp.int32, (8, 128), 0)
-    up = pltpu.roll(pltpu.roll(x, 1, 1), 1, 0)
-    down = pltpu.roll(pltpu.roll(x, 127, 1), 7, 0)
-    x = x + jnp.where((sub == 0) & (lane != 0), up, 0.0)
-    return x + jnp.where((sub == 7) & (lane != 31), down, 0.0)
-
-
-def assemble_inside(h_ref, x_ref):
-    def part(n, carry):
-        f, a = n // 2, n % 2
-        lanes = pl.ds(pl.multiple_of(a * 128, 128), 128)
-        for i in range(1, 7):
-            for j in range(1, 7):
-                row = pl.ds(i * 64 + j * 8, 8)
-                x_ref[f, row, lanes] = radially(h_ref[f, row, lanes])
-        return carry
-
-    lax.fori_loop(0, 6, part, 0)
-
-
-def assemble_rim(h_ref, x_ref, low_ref, high_ref, left_ref, right_ref, corner_ref, lowest, highest):
-    quarter = lax.broadcasted_iota(jnp.int32, (8, 128), 1) // 32
+def assemble(h_ref, low_ref, high_ref, left_ref, right_ref, corner_ref, lowest, highest):
+    lane = lax.broadcasted_iota(jnp.int32, (8, 128), 1)
+    quarter, radial = lane // 32, lane % 32
     under = jnp.where(lowest, F32(0.0), F32(1.0))
     over = jnp.where(highest, F32(0.0), F32(1.0))
 
@@ -315,8 +277,8 @@
         def corner(n, q, turn, scale):
             return jnp.where(quarter == q, pltpu.roll(corner_ref[n, f], turn, 1) * scale, 0.0)
 
-        h_ref[f, 0:64, 0:128] += low_ref[f] * under
-        h_ref[f, 448:512, 128:256] += high_ref[f] * over
+        h_ref[2 * f, 0:64] += low_ref[f] * under
+        h_ref[2 * f + 1, 448:512] += high_ref[f] * over
         left_ref[f, 0, 0] += corner(0, 0, 32, under)
         left_ref[f, 1, 1] += corner(1, 3, 96, over)
         right_ref[f, 0, 0] += corner(2, 0, 32, under)
@@ -327,11 +289,10 @@
 
     def part(n, carry):
         f, a = n // 2, n % 2
-        lanes = pl.ds(pl.multiple_of(a * 128, 128), 128)
         for i in range(8):
             half, q = i // 4, i % 4
-            first = h_ref[f, pl.ds(i * 64, 8), lanes]
-            last = h_ref[f, pl.ds(i * 64 + 56, 8), lanes]
+            first = h_ref[n, pl.ds(i * 64, 8), :]
+            last = h_ref[n, pl.ds(i * 64 + 56, 8), :]
             before, after = left_ref[f, a, half], right_ref[f, a, half]
             if q:
                 before = pltpu.roll(before, 128 - 32 * q, 1)
@@ -339,12 +300,13 @@
                 after = pltpu.roll(after, 96 - 32 * q, 1)
             before = jnp.where(quarter == 0, before, pltpu.roll(last, 32, 1))
             after = jnp.where(quarter == 3, after, pltpu.roll(first, 96, 1))
-            x_ref[f, pl.ds(i * 64, 8), lanes] = radially(first + before)
-            x_ref[f, pl.ds(i * 64 + 56, 8), lanes] = radially(last + after)
-        for i in (0, 7):
-            for j in range(1, 7):
-                row = pl.ds(i * 64 + j * 8, 8)
-                x_ref[f, row, lanes] = radially(h_ref[f, row, lanes])
+            h_ref[n, pl.ds(i * 64, 8), :] = first + before
+            h_ref[n, pl.ds(i * 64 + 56, 8), :] = last + after
+        for i in range(8):
+            inner, outer = pl.ds(i * 64, 8, stride=8), pl.ds(i * 64 + 7, 8, stride=8)
+            first, last = h_ref[n, inner, :], h_ref[n, outer, :]
+            h_ref[n, inner, :] = first + jnp.where(radial != 0, pltpu.roll(last, 1, 1), 0.0)
+            h_ref[n, outer, :] = last + jnp.where(radial != 31, pltpu.roll(first, 127, 1), 0.0)
         return carry
 
     lax.fori_loop(0, 6, part, 0)
@@ -354,13 +316,13 @@
     def three(d, carry):
         for a in range(2):
             lanes = pl.ds(a * 128, 128)
-            out_ref[d, lanes, :] = jnp.transpose(x_ref[d, :, lanes])
+            out_ref[d, lanes, :] = jnp.transpose(x_ref[d * 2 + a])
         return carry
 
     lax.fori_loop(0, 3, three, 0)
 
 
-FIELD = ((3, 512, 256), F32)
+FIELD = ((6, 512, 128), F32)
 FACE = ((3, 64, 128), F32)
 SIDE = ((3, 2, 2, 8, 128), F32)
 CORNER = ((4, 3, 8, 128), F32)
@@ -397,25 +359,21 @@
 
 
 def main_body(n_ax, n_xs, *refs):
-    (flow_h, heat_h, stiff_h, inert_h, idx_h, off_h, own_h, piece_h) = refs[:8]
-    turned, probe, coords = refs[8:11]
-    (flow, heat, stiff, inert, idx, off, own, piece) = refs[11:19]
-    (rank, pay, got, back, ret, x, h, g, c, table, tables, lag, halves) = refs[19:32]
-    (low1, high1, left1, right1, low2, high2, left2, right2, corners1) = refs[32:41]
-    (low3, high3, left3, right3, low4, high4, left4, right4, corners2) = refs[41:50]
-    (in_sems, out_send, out_recv, back_send, back_recv, rim_send, rim_recv) = refs[50:]
+    sources = refs[:11]
+    turned, cnew, snew = refs[11:14]
+    held = refs[14:25]
+    (idx, off, own, piece, flow, heat, stiff, inert, share, freq, energy) = held
+    (rank, pay, got, back, ret, x, h, g, c, table, lag, halves, probe, coords) = refs[25:39]
+    (low1, high1, left1, right1, low2, high2, left2, right2, corners1) = refs[39:48]
+    (low3, high3, left3, right3, low4, high4, left4, right4, corners2) = refs[48:57]
+    (in_sems, out_send, out_recv, back_send, back_recv, rim_send, rim_recv) = refs[57:]
     devices = n_ax * n_xs
     ax, xs = lax.axis_index("ax"), lax.axis_index("xs")
     me = ax * n_xs + xs
 
     loads = [
         pltpu.make_async_copy(src, dst, in_sems.at[n])
-        for n, (src, dst) in enumerate(
-            zip(
-                (idx_h, off_h, own_h, piece_h, flow_h, heat_h, stiff_h, inert_h),
-                (idx, off, own, piece, flow, heat, stiff, inert),
-            )
-        )
+        for n, (src, dst) in enumerate(zip(sources, held))
     ]
     for load in loads:
         load.start()
@@ -432,33 +390,39 @@
         return carry
 
     lax.fori_loop(1, devices, greet, 0)
-    fill_tables(tables)
     for load in loads[:4]:
         load.wait()
     dispatch(idx, off, own, piece, coords, rank, pay)
+    for load in loads[4:]:
+        load.wait()
+    turn_in(flow, heat, stiff, inert, x, table, g, c)
     pl.semaphore_wait(barrier, devices - 1)
 
     own_copy = pltpu.make_async_copy(pay.at[me], got.at[me], out_recv.at[ax])
     own_copy.start()
 
-    def send(k, carry):
-        to = lax.rem(me + k, devices)
+    def send_to(row, column):
         pltpu.make_async_remote_copy(
-            src_ref=pay.at[to],
+            src_ref=pay.at[row * n_xs + column],
             dst_ref=got.at[me],
             send_sem=out_send,
             recv_sem=out_recv.at[ax],
-            device_id=where(to),
+            device_id=(row, column),
             device_id_type=MESH,
         ).start()
-        return carry
-
-    lax.fori_loop(1, devices, send, 0)
-
-    for load in loads[4:]:
-        load.wait()
-    turn_in(flow, heat, stiff, inert, x, table, g, c)
-    helm(x, g, c, tables, h)
+
+    for dx in range(1, n_xs):
+        send_to(ax, lax.rem(xs + dx, n_xs))
+
+    def send(da, carry):
+        row = lax.rem(ax + da, n_ax)
+        for dx in range(n_xs):
+            send_to(row, lax.rem(xs + dx, n_xs))
+        return carry
+
+    lax.fori_loop(1, n_ax, send, 0)
+
+    helm(x, g, c, h)
     faces(h, low1, high1, left1, right1)
     first = rim_copies(
         n_ax, n_xs, (low1, high1, left1, right1), (low2, high2, left2, right2), corners1,
@@ -475,36 +439,36 @@
         for part in range(n_xs // 8):
             interpolate(base + part * 8, got, table, back, lag.at[part])
 
-        def give(s, inner):
-            to = base + s
-
-            @pl.when(to != me)
-            def _():
-                pltpu.make_async_remote_copy(
-                    src_ref=back.at[to],
-                    dst_ref=ret.at[me],
-                    send_sem=back_send,
-                    recv_sem=back_recv,
-                    device_id=(now, s),
-                    device_id_type=MESH,
-                ).start()
-
-            @pl.when(to == me)
-            def _():
-                pltpu.make_async_copy(back.at[to], ret.at[me], back_recv).start()
-
-            return inner
-
-        lax.fori_loop(0, n_xs, give, 0)
+        def give(to, row, column):
+            pltpu.make_async_remote_copy(
+                src_ref=back.at[to],
+                dst_ref=ret.at[me],
+                send_sem=back_send,
+                recv_sem=back_recv,
+                device_id=(row, column),
+                device_id_type=MESH,
+            ).start()
+
+        @pl.when(now != ax)
+        def _():
+            for column in range(n_xs):
+                give(base + column, now, column)
+
+        @pl.when(now == ax)
+        def _():
+            for step in range(1, n_xs):
+                column = lax.rem(xs + step, n_xs)
+                give(base + column, ax, column)
+            pltpu.make_async_copy(back.at[me], ret.at[me], back_recv).start()
+
         return carry
 
     lax.fori_loop(0, n_ax // 4, block, 0)
-    assemble_inside(h, x)
     for copy in first:
         copy.wait()
-    assemble_rim(h, x, low2, high2, left2, right2, corners1, ax == 0, ax == n_ax - 1)
-    helm(x, g, c, tables, h)
-    faces(h, low3, high3, left3, right3)
+    assemble(h, low2, high2, left2, right2, corners1, ax == 0, ax == n_ax - 1)
+    helm(h, g, c, x)
+    faces(x, low3, high3, left3, right3)
     second = rim_copies(
         n_ax, n_xs, (low3, high3, left3, right3), (low4, high4, left4, right4), corners2,
         rim_send.at[1], rim_recv.at[1],
@@ -513,24 +477,25 @@
         copy.start()
     lax.fori_loop(n_ax // 4, n_ax, block, 0)
 
-    assemble_inside(h, x)
     for copy in second:
         copy.wait()
-    assemble_rim(h, x, low4, high4, left4, right4, corners2, ax == 0, ax == n_ax - 1)
+    assemble(x, low4, high4, left4, right4, corners2, ax == 0, ax == n_ax - 1)
     turn_out(x, turned)
     pltpu.make_async_copy(ret, ret, back_recv).wait()
     gather_back(ret, own, rank, probe, halves)
+    kinetics(probe, coords, share, freq, energy, cnew, snew)
 
     others = pl.ds(0, devices - 1)
     pltpu.make_async_copy(pay.at[others], pay.at[others], out_send).wait()
     pltpu.make_async_copy(back.at[others], back.at[others], back_send).wait()
 
 
-def last_body(turned, probe, coords, shares, freq, barrier, out, cnew, snew, sem):
-    copy = pltpu.make_async_copy(turned, out, sem)
-    copy.start()
-    kinetics(probe, coords, shares, freq, barrier, cnew, snew)
-    copy.wait()
+def last_body(*refs):
+    copies = [pltpu.make_async_copy(refs[n], refs[3 + n], refs[6].at[n]) for n in range(3)]
+    for copy in copies:
+        copy.start()
+    for copy in copies:
+        copy.wait()
 
 
 def shapes(outs):
@@ -547,32 +512,36 @@
     devices = n_ax * n_xs
     vmem = pl.BlockSpec(memory_space=pltpu.VMEM)
     hbm = pl.BlockSpec(memory_space=pltpu.HBM)
-    smem = pl.BlockSpec(memory_space=pltpu.SMEM)
     inputs = (
+        index,
+        offset,
+        owner.reshape(1, particles),
+        piece.reshape(1, particles),
         flow.reshape(3, 256, 512),
         heat.reshape(256, 512),
         stiff.reshape(3, 256, 512),
         inert.reshape(256, 512),
-        index,
-        offset,
-        owner.reshape(1, particles),
-        piece.reshape(1, particles),
+        shares,
+        freq,
+        barrier,
     )
     inputs = [pltpu.with_memory_space_constraint(a, pltpu.HBM) for a in inputs]
     held = [(a.shape, a.dtype) for a in inputs]
     table = ((2048, 256), BF16)
-    outs = [((3, 256, 512), F32), ((4, particles), F32), ((3, particles), F32)]
+    outs = [((3, 256, 512), F32), ((3, particles), F32), ((6, particles), F32)]
     passed = pl.pallas_call(
         functools.partial(main_body, n_ax, n_xs),
         out_shape=shapes(outs),
-        in_specs=[hbm] * 8,
+        in_specs=[hbm] * 11,
         out_specs=[vmem] * len(outs),
-        scratch_shapes=buffers(held)
+        scratch_shapes=buffers(held[:9])
+        + [pltpu.SMEM(*one) for one in held[9:]]
         + buffers([((1, particles), jnp.int32), SLOTS, SLOTS, SLOTS, SLOTS, FIELD, FIELD, FIELD])
-        + buffers([((512, 256), F32), table, ((16, 8, 128), F32), ((2, 192, 128), F32), ((512, 256), BF16)])
+        + buffers([((2, 512, 128), F32), table, ((2, 192, 128), F32), ((512, 256), BF16)])
+        + buffers([((4, particles), F32), ((3, particles), F32)])
         + buffers([*RIMS, *RIMS, CORNER, *RIMS, *RIMS, CORNER])
         + [
-            pltpu.SemaphoreType.DMA((8,)),
+            pltpu.SemaphoreType.DMA((11,)),
             pltpu.SemaphoreType.DMA,
             pltpu.SemaphoreType.DMA((n_ax,)),
             pltpu.SemaphoreType.DMA,
@@ -584,15 +553,14 @@
             collective_id=0, has_side_effects=True, vmem_limit_bytes=LIMIT
         ),
     )(*inputs)
-    outs = [((3, 256, 512), F32), ((3, particles), F32), ((6, particles), F32)]
     out, cnew, snew = pl.pallas_call(
         last_body,
         out_shape=shapes(outs),
-        in_specs=[vmem] * 4 + [smem] * 2,
-        out_specs=[hbm, vmem, vmem],
-        scratch_shapes=[pltpu.SemaphoreType.DMA],
+        in_specs=[vmem] * 3,
+        out_specs=[hbm] * 3,
+        scratch_shapes=[pltpu.SemaphoreType.DMA((3,))],
         compiler_params=pltpu.CompilerParams(vmem_limit_bytes=8 * 1024 * 1024),
-    )(*passed, shares, freq, barrier)
+    )(*passed)
     return out.reshape(flow.shape), cnew, snew
 
 

time: 57.9 us -> 51.9 us (0.90)
  Pallas kernels: 57.1 us -> 50.9 us
    pallas_call x1, Pallas kernels: 54.8 us -> 49.7 us  [local(): pl.pallas_call(functools.partial(main_body, n_ax, n_xs), out_shape=shapes...]
    pallas_call x1, Pallas kernels: 2.37 us -> 1.22 us  [local(): pl.pallas_call(last_body, out_shape=shapes(outs), in_specs=[vmem] * 3, ou...]
where the time goes in v4:
time: 51.9 us; the launch traced here: 51.5 us
  Pallas kernels  50.9 us (98%)
  between operations  0.64 us (1%)
    pallas_call x1, Pallas kernels, local(): pl.pallas_call(functools.partial(main_body, n_ax, n_xs), out_shape=shapes...  49.7 us
    pallas_call x1, Pallas kernels, local(): pl.pallas_call(last_body, out_shape=shapes(outs), in_specs=[vmem] * 3, ou...  1.22 us

profile of v4, /device:TPU:1, one launch (start us, length us, event | category | flops | bytes accessed | tf_op | source)
XLA Modules:
  0.0 51.5 jit_solution(17773874390732691191)
XLA Ops:
  0.6 49.7 %shard_map.130 = (f32[3,256,512]{2,1,0:T(8,128)S(1)}, f32[3,4096]{1,0:T(4,128)S(1)}, f32[6,4096]{1,0:T(8,128)S(1)}) custom-call(s32[3,4096]{1,0:T(4,128)} %refs_0_.1, f32[3,4096]{1,0:T(4,128)} %refs_1_.1, s32[1,4096]{1,0:T(1,128)} %bitcast.11, s32[1,4096]{1,0:T(1,128)} %bitcast.12, bf16[3,256,512]{2,1,0:T(8,128)(2,1)} %bitcast.8, bf16[256,512]{1,0:T(8,128)(2,1)} %bitcast.10, ...), custom_call_target="tpu_custom_call" | custom-call | tf_op jit(solution)/shard_map/pallas_call | solution.py:532
  50.3 1.2 %shard_map.131 = (f32[3,256,512]{2,1,0:T(8,128)}, f32[3,4096]{1,0:T(4,128)}, f32[6,4096]{1,0:T(8,128)}) custom-call(f32[3,256,512]{2,1,0:T(8,128)S(1)} %get-tuple-element.9.refs_0_, f32[3,4096]{1,0:T(4,128)S(1)} %get-tuple-element.10.refs_1_, f32[6,4096]{1,0:T(8,128)S(1)} %get-tuple-element.11.refs_2_), custom_call_target="tpu_custom_call" | custom-call | tf_op jit(solution)/shard_map/pallas_call | solution.py:556

commit v5 on v4

--- a/solution.py
+++ b/solution.py
@@ -267,22 +267,20 @@
     lax.fori_loop(0, 6, pack, 0)
 
 
-def assemble(h_ref, low_ref, high_ref, left_ref, right_ref, corner_ref, lowest, highest):
+def assemble(h_ref, low_ref, high_ref, left_ref, right_ref, corner_ref):
     lane = lax.broadcasted_iota(jnp.int32, (8, 128), 1)
     quarter, radial = lane // 32, lane % 32
-    under = jnp.where(lowest, F32(0.0), F32(1.0))
-    over = jnp.where(highest, F32(0.0), F32(1.0))
 
     def near(f, carry):
-        def corner(n, q, turn, scale):
-            return jnp.where(quarter == q, pltpu.roll(corner_ref[n, f], turn, 1) * scale, 0.0)
-
-        h_ref[2 * f, 0:64] += low_ref[f] * under
-        h_ref[2 * f + 1, 448:512] += high_ref[f] * over
-        left_ref[f, 0, 0] += corner(0, 0, 32, under)
-        left_ref[f, 1, 1] += corner(1, 3, 96, over)
-        right_ref[f, 0, 0] += corner(2, 0, 32, under)
-        right_ref[f, 1, 1] += corner(3, 3, 96, over)
+        def corner(n, q, turn):
+            return jnp.where(quarter == q, pltpu.roll(corner_ref[n, f], turn, 1), 0.0)
+
+        h_ref[2 * f, 0:64] += low_ref[f]
+        h_ref[2 * f + 1, 448:512] += high_ref[f]
+        left_ref[f, 0, 0] += corner(0, 0, 32)
+        left_ref[f, 1, 1] += corner(1, 3, 96)
+        right_ref[f, 0, 0] += corner(2, 0, 32)
+        right_ref[f, 1, 1] += corner(3, 3, 96)
         return carry
 
     lax.fori_loop(0, 3, near, 0)
@@ -345,7 +343,7 @@
         (left.at[:, 1, 1], corners.at[2], 1, -1),
         (left.at[:, 0, 0], corners.at[3], -1, -1),
     ]
-    return [
+    copies = [
         pltpu.make_async_remote_copy(
             src_ref=src,
             dst_ref=dst,
@@ -356,6 +354,24 @@
         )
         for n, (src, dst, da, dx) in enumerate(plan)
     ]
+    below, above = ax > 0, ax < n_ax - 1
+
+    def each(da, there, action):
+        if da == 0:
+            action()
+        else:
+            pl.when(above if da == there else below)(action)
+
+    def start():
+        for copy, (_, _, da, _) in zip(copies, plan):
+            each(da, 1, copy.start)
+
+    def wait():
+        for copy, (_, _, da, _) in zip(copies, plan):
+            each(da, 1, copy.wait_send)
+            each(da, -1, copy.wait_recv)
+
+    return start, wait
 
 
 def main_body(n_ax, n_xs, *refs):
@@ -390,6 +406,21 @@
         return carry
 
     lax.fori_loop(1, devices, greet, 0)
+
+    @pl.when(ax == 0)
+    def _():
+        for low, corners in ((low2, corners1), (low4, corners2)):
+            low[...] = jnp.zeros_like(low)
+            corners[0] = jnp.zeros((3, 8, 128), F32)
+            corners[2] = jnp.zeros((3, 8, 128), F32)
+
+    @pl.when(ax == n_ax - 1)
+    def _():
+        for high, corners in ((high2, corners1), (high4, corners2)):
+            high[...] = jnp.zeros_like(high)
+            corners[1] = jnp.zeros((3, 8, 128), F32)
+            corners[3] = jnp.zeros((3, 8, 128), F32)
+
     for load in loads[:4]:
         load.wait()
     dispatch(idx, off, own, piece, coords, rank, pay)
@@ -411,16 +442,15 @@
             device_id_type=MESH,
         ).start()
 
+    def send(da, carry):
+        row = lax.rem(ax + n_ax - da, n_ax)
+        for dx in range(n_xs):
+            send_to(row, lax.rem(xs + dx, n_xs))
+        return carry
+
+    lax.fori_loop(1, n_ax, send, 0)
     for dx in range(1, n_xs):
         send_to(ax, lax.rem(xs + dx, n_xs))
-
-    def send(da, carry):
-        row = lax.rem(ax + da, n_ax)
-        for dx in range(n_xs):
-            send_to(row, lax.rem(xs + dx, n_xs))
-        return carry
-
-    lax.fori_loop(1, n_ax, send, 0)
 
     helm(x, g, c, h)
     faces(h, low1, high1, left1, right1)
@@ -428,11 +458,10 @@
         n_ax, n_xs, (low1, high1, left1, right1), (low2, high2, left2, right2), corners1,
         rim_send.at[0], rim_recv.at[0],
     )
-    for copy in first:
-        copy.start()
+    first[0]()
 
     def block(n, carry):
-        now = lax.rem(ax + 2 * n_ax - 1 - n, n_ax)
+        now = lax.rem(ax + 1 + n, n_ax)
         base = now * n_xs
         rows = got.at[pl.ds(base, n_xs)]
         pltpu.make_async_copy(rows, rows, out_recv.at[now]).wait()
@@ -464,22 +493,19 @@
         return carry
 
     lax.fori_loop(0, n_ax // 4, block, 0)
-    for copy in first:
-        copy.wait()
-    assemble(h, low2, high2, left2, right2, corners1, ax == 0, ax == n_ax - 1)
+    first[1]()
+    assemble(h, low2, high2, left2, right2, corners1)
     helm(h, g, c, x)
     faces(x, low3, high3, left3, right3)
     second = rim_copies(
         n_ax, n_xs, (low3, high3, left3, right3), (low4, high4, left4, right4), corners2,
         rim_send.at[1], rim_recv.at[1],
     )
-    for copy in second:
-        copy.start()
+    second[0]()
     lax.fori_loop(n_ax // 4, n_ax, block, 0)
 
-    for copy in second:
-        copy.wait()
-    assemble(x, low4, high4, left4, right4, corners2, ax == 0, ax == n_ax - 1)
+    second[1]()
+    assemble(x, low4, high4, left4, right4, corners2)
     turn_out(x, turned)
     pltpu.make_async_copy(ret, ret, back_recv).wait()
     gather_back(ret, own, rank, probe, halves)

time: 51.9 us -> 52.1 us (level)
  no operation moved by 1% of the time
where the time goes in v5:
time: 52.1 us; the launch traced here: 51.9 us
  Pallas kernels  51.1 us (98%)
  between operations  0.8 us (2%)
    pallas_call x1, Pallas kernels, local(): pl.pallas_call(functools.partial(main_body, n_ax, n_xs), out_shape=shapes...  49.9 us
    pallas_call x1, Pallas kernels, local(): pl.pallas_call(last_body, out_shape=shapes(outs), in_specs=[vmem] * 3, ou...  1.22 us

profile of v5, /device:TPU:1, one launch (start us, length us, event | category | flops | bytes accessed | tf_op | source)
XLA Modules:
  0.0 51.9 jit_solution(9665480019244839600)
XLA Ops:
  0.6 49.9 %shard_map.130 = (f32[3,256,512]{2,1,0:T(8,128)S(1)}, f32[3,4096]{1,0:T(4,128)S(1)}, f32[6,4096]{1,0:T(8,128)S(1)}) custom-call(s32[3,4096]{1,0:T(4,128)} %refs_0_.1, f32[3,4096]{1,0:T(4,128)} %refs_1_.1, s32[1,4096]{1,0:T(1,128)} %bitcast.11, s32[1,4096]{1,0:T(1,128)} %bitcast.12, bf16[3,256,512]{2,1,0:T(8,128)(2,1)} %bitcast.8, bf16[256,512]{1,0:T(8,128)(2,1)} %bitcast.10, ...), custom_call_target="tpu_custom_call" | custom-call | tf_op jit(solution)/shard_map/pallas_call | solution.py:558
  50.6 1.2 %shard_map.131 = (f32[3,256,512]{2,1,0:T(8,128)}, f32[3,4096]{1,0:T(4,128)}, f32[6,4096]{1,0:T(8,128)}) custom-call(f32[3,256,512]{2,1,0:T(8,128)S(1)} %get-tuple-element.9.refs_0_, f32[3,4096]{1,0:T(4,128)S(1)} %get-tuple-element.10.refs_1_, f32[6,4096]{1,0:T(8,128)S(1)} %get-tuple-element.11.refs_2_), custom_call_target="tpu_custom_call" | custom-call | tf_op jit(solution)/shard_map/pallas_call | solution.py:582
